TPU v7x, 256 devices: a whole 4x4x8 slice. The times are simulated.
256 devices in a mesh: sta: 64 (over z, x, y_lo), day: 4 (over y_hi, core).
Axes of the slice: x: 4, y: 4 (y_hi: 2, y_lo: 2; y = y_hi * 2 + y_lo), z: 8, core: 2. Of those that a mesh axis runs over, the one named last changes fastest.
Arguments:
- spectra: bfloat16 [512, 32, 2, 640], P('sta', 'day'), may hold values from -80 to 80
- pairing: int32 [3, 64], replicated, may hold values from 0 to 63, as said below
- station_slot: int32 [512], replicated, may hold values from 0 to 7, as said below
Outputs:
- correlations: bfloat16 [3, 8, 512, 512], P(None, 'day', 'sta')
Inputs may be any that keep to these rules, and one draw needn't show every extreme that they name: In every round the table is a perfect matching of the 64 blocks: block b meets pairing[r, b], which meets b back, never b itself; no two blocks meet in two rounds. `station_slot`: within every block of 8 consecutive stations each slot from 0 to 7 appears once.
All inputs are finite; a program needn't handle non-finite values.
Results may differ from a plain program's by a relative error of at most 0.001.
Values may be sent and summed in bfloat16 or wider, within the bound.
A program may use at most 64 MiB of HBM per device.

v0:
```python
import jax
import jax.numpy as jnp
from jax import lax
from jax.sharding import PartitionSpec as P

BIN_LO = 60
SEGLEN = 6000
LAGS = 512
ROUNDS = 3


EPS = 1e-06


def lag_table(nfreq, lags):
    bins = BIN_LO + jnp.arange(nfreq, dtype=jnp.int32)
    shifts = jnp.arange(lags, dtype=jnp.int32) - lags // 2
    turns = jnp.mod(bins[:, None] * shifts[None, :], SEGLEN).astype(jnp.float32)
    angle = 2.0 * jnp.pi / SEGLEN * turns
    return jnp.concatenate([jnp.cos(angle), -jnp.sin(angle)], axis=0)


def cross_spectrum(own, other):
    own_re = own[:, :, 0, :].astype(jnp.float32)
    own_im = own[:, :, 1, :].astype(jnp.float32)

    def one_partner(single):
        other_re = single[:, 0, :].astype(jnp.float32)[None]
        other_im = single[:, 1, :].astype(jnp.float32)[None]
        real_part = jnp.sum(own_re * other_re + own_im * other_im, axis=1)
        imag_part = jnp.sum(own_im * other_re - own_re * other_im, axis=1)
        return jnp.concatenate([real_part, imag_part], axis=1)

    return lax.map(one_partner, other)


def per_device(spectra, pairing, station_slot):
    own_rows, seg_dev, _, nfreq = spectra.shape
    day_count = lax.axis_size("day")
    blocks = lax.axis_size("sta")
    own_block = lax.axis_index("sta")
    day_index = lax.axis_index("day")
    rows_kept = own_rows // day_count
    segs_total = seg_dev * day_count
    squares = jnp.sum(jnp.square(spectra.astype(jnp.float32)), axis=(1, 2, 3))
    summed = lax.psum(squares, "day")
    energy_all = (
        lax.all_gather(summed, "sta", axis=0, tiled=True) / float(segs_total * 2 * nfreq) + EPS
    )
    slot_order = jnp.argsort(station_slot.reshape(blocks, own_rows), axis=1)
    table = lag_table(nfreq, LAGS)
    scale = jnp.sqrt(jnp.float32(2 * nfreq * segs_total))
    energy_i = lax.dynamic_slice_in_dim(energy_all, own_block * own_rows, own_rows)
    results = []
    for round_index in range(ROUNDS):
        banded = lax.all_to_all(spectra, "sta", split_axis=3, concat_axis=0, tiled=True)
        partner_row = pairing[round_index]
        picked = banded.reshape(blocks, own_rows, seg_dev, 2, -1)[partner_row]
        reorder = slot_order[partner_row]
        picked = jnp.take_along_axis(picked, reorder[:, :, None, None, None], axis=1)
        partner = lax.all_to_all(
            picked.reshape(blocks * own_rows, seg_dev, 2, -1),
            "sta",
            split_axis=0,
            concat_axis=3,
            tiled=True,
        )
        cross = cross_spectrum(spectra, partner)
        product = jnp.dot(
            cross.reshape(rows_kept * lax.axis_size("day") * own_rows, -1),
            table,
            precision=lax.Precision.HIGHEST,
        )
        raw = lax.psum_scatter(
            product.reshape(rows_kept * lax.axis_size("day"), own_rows, LAGS),
            "day",
            scatter_dimension=0,
            tiled=True,
        )
        partner_block = partner_row[own_block]
        partner_order = lax.dynamic_slice_in_dim(
            slot_order[partner_block], day_index * rows_kept, rows_kept
        )
        energy_j = energy_all[partner_block * own_rows + partner_order]
        result = raw / jnp.sqrt(energy_j[:, None, None] * energy_i[None, :, None]) / scale
        results.append(result.astype(jnp.bfloat16))
    return jnp.stack(results)


def solution(mesh):
    in_specs = (P("sta", "day", None, None), P(), P())
    out_specs = P(None, "day", "sta", None)
    return jax.shard_map(
        per_device, mesh=mesh, in_specs=in_specs, out_specs=out_specs, check_vma=False
    )
```

profile of v0, /device:TPU:1, one launch (start us, length us, event | category | flops | bytes accessed | tf_op | source)
XLA Modules:
  0.0 484.2 jit_solution(3728108522144333447)
XLA Ops:
  6.5 5.0 %copy.57 = bf16[8,8,2,640]{1,0,2,3:T(8,128)(2,1)S(1)} copy(bf16[8,8,2,640]{3,2,1,0:T(2,128)(2,1)} %param.11) | data formatting | bytes 327680 | tf_op args[0]
  11.6 3.4 reshape.493
  15.0 13.5 %all-to-all-start = ((bf16[64,2,640]{2,1,0:T(2,128)(2,1)}), bf16[64,2,640]{2,1,0:T(2,128)(2,1)S(1)}, u32[]{:S(2)}, u32[]{:S(2)}) async-start(bf16[64,2,640]{2,1,0:T(2,128)(2,1)} %reshape.493), calls=%async_computation | async-start | bytes 327680 | tf_op jit(solution)/shard_map/all_to_all | solution.py:56
  41.6 7.5 %psum.7 = f32[8]{0:T(128)S(1)} all-reduce(f32[8]{0:T(128)S(1)} %multiply_reduce_fusion), channel_id=1, replica_groups=mesh['sta'=64,'day'=4] {'day'}, use_global_device_ids=true, to_apply=%region_7.9 | all-reduce | flops 8 | bytes 64 | tf_op jit(solution)/shard_map/psum | solution.py:46
  50.6 131.3 %all-reduce = f32[512]{0:T(512)S(1)} all-reduce(f32[512]{0:T(512)S(1)} %dynamic-update-slice), channel_id=1, replica_groups=mesh['sta'=64,'day'=4] {'sta'}, use_global_device_ids=true, to_apply=%add | all-reduce | flops 512 | bytes 4096
  184.4 6.8 %fusion.16 = (f32[640,512]{1,0:T(8,128)}, f32[640,512]{1,0:T(8,128)}) fusion(s32[512]{0:T(512)S(1)} %iota_add_fusion.1, s32[640]{0:T(1024)S(1)} %iota_add_fusion), kind=kLoop, calls=%fused_computation.53 | loop fusion | flops 3276800 | bytes 2626048 | tf_op jit(solution)/shard_map/cos | solution.py:20
  191.2 4.2 reshape.494
  195.4 7.4 %copy.59 = bf16[8,8,2,64,10]{4,1,2,0,3:T(8,128)(2,1)S(1)} copy(bf16[8,8,2,64,10]{1,0,2,4,3:T(8,128)(2,1)} %bitcast.197) | data formatting | bytes 327680 | tf_op jit(solution)/shard_map/all_to_all | solution.py:56
  202.8 2.2 gather_fusion.3
  205.0 2.2 gather_fusion
  207.1 2.1 gather_fusion.6
  209.3 7.0 %gather_fusion.10 = bf16[512,8,2,10]{3,1,2,0:T(8,128)(2,1)} fusion(bf16[64,8,8,2,10]{4,2,3,1,0:T(8,128)(2,1)} %gather_fusion.3, s32[512]{0:T(512)S(1)} %reshape.480), kind=kCustom, calls=%fused_computation.1.clone | custom fusion | bytes 331776 | tf_op jit(solution)/shard_map/jit(take_along_axis)/gather | solution.py:60
  216.3 8.9 %copy.67 = bf16[64,8,8,2,10]{1,0,2,4,3:T(8,128)(2,1)S(1)} copy(bf16[64,8,8,2,10]{4,2,3,1,0:T(8,128)(2,1)} %bitcast.199) | data formatting | bytes 327680 | tf_op jit(solution)/shard_map/jit(take_along_axis)/gather | solution.py:60
  225.2 1.7 broadcast_select_fusion.1
  226.9 8.7 %copy.81 = bf16[64,8,8,2,10]{4,2,3,1,0:T(8,128)(2,1)} copy(bf16[64,8,8,2,10]{1,0,2,4,3:T(8,128)(2,1)} %broadcast_select_fusion.1) | data formatting | bytes 327680 | tf_op jit(solution)/shard_map/reshape | solution.py:62
  235.6 5.1 %reshape.497 = bf16[64,2,640]{2,1,0:T(2,128)(2,1)} reshape(bf16[512,2,8,10]{3,2,1,0:T(8,128)(2,1)} %bitcast.202) | data formatting | bytes 327680
  240.7 5.1 %all-to-all-start.2 = ((bf16[64,2,640]{2,1,0:T(2,128)(2,1)}), bf16[64,2,640]{2,1,0:T(2,128)(2,1)S(1)}, u32[]{:S(2)}, u32[]{:S(2)}) async-start(bf16[64,2,640]{2,1,0:T(2,128)(2,1)} %reshape.497), calls=%async_computation.3 | async-start | bytes 327680 | tf_op jit(solution)/shard_map/all_to_all | solution.py:61
  245.8 5.4 %gather_fusion.9 = bf16[512,8,2,10]{3,1,2,0:T(8,128)(2,1)} fusion(bf16[64,8,8,2,10]{4,2,3,1,0:T(8,128)(2,1)S(1)} %copy-done.3, s32[512]{0:T(512)S(1)} %reshape.475), kind=kCustom, calls=%fused_computation.clone | custom fusion | bytes 331776 | tf_op jit(solution)/shard_map/jit(take_along_axis)/gather | solution.py:60
  251.2 8.8 %copy.60 = bf16[64,8,8,2,10]{1,0,2,4,3:T(8,128)(2,1)S(1)} copy(bf16[64,8,8,2,10]{4,2,3,1,0:T(8,128)(2,1)} %bitcast.200) | data formatting | bytes 327680 | tf_op jit(solution)/shard_map/jit(take_along_axis)/gather | solution.py:60
  260.1 1.7 broadcast_select_fusion.2
  261.8 8.6 %copy.78 = bf16[64,8,8,2,10]{4,2,3,1,0:T(8,128)(2,1)} copy(bf16[64,8,8,2,10]{1,0,2,4,3:T(8,128)(2,1)} %broadcast_select_fusion.2) | data formatting | bytes 327680 | tf_op jit(solution)/shard_map/reshape | solution.py:62
  270.4 5.1 %reshape.499 = bf16[64,2,640]{2,1,0:T(2,128)(2,1)} reshape(bf16[512,2,8,10]{3,2,1,0:T(8,128)(2,1)} %bitcast.203) | data formatting | bytes 327680
  275.5 5.4 %gather_fusion.11 = bf16[512,8,2,10]{3,1,2,0:T(8,128)(2,1)} fusion(bf16[64,8,8,2,10]{4,2,3,1,0:T(8,128)(2,1)S(1)} %copy-done.2, s32[512]{0:T(512)S(1)} %reshape.485), kind=kCustom, calls=%fused_computation.2.clone | custom fusion | bytes 331776 | tf_op jit(solution)/shard_map/jit(take_along_axis)/gather | solution.py:60
  280.9 8.9 %copy.72 = bf16[64,8,8,2,10]{1,0,2,4,3:T(8,128)(2,1)S(1)} copy(bf16[64,8,8,2,10]{4,2,3,1,0:T(8,128)(2,1)} %bitcast.201) | data formatting | bytes 327680 | tf_op jit(solution)/shard_map/jit(take_along_axis)/gather | solution.py:60
  289.8 1.7 broadcast_select_fusion
  291.6 7.9 %copy.84 = bf16[64,8,8,2,10]{4,2,3,1,0:T(8,128)(2,1)S(1)} copy(bf16[64,8,8,2,10]{1,0,2,4,3:T(8,128)(2,1)} %broadcast_select_fusion) | data formatting | bytes 327680 | tf_op jit(solution)/shard_map/reshape | solution.py:62
  299.5 4.3 reshape.495
  303.8 10.8 %all-to-all-start.1 = ((bf16[64,2,640]{2,1,0:T(2,128)(2,1)}), bf16[64,2,640]{2,1,0:T(2,128)(2,1)S(1)}, u32[]{:S(2)}, u32[]{:S(2)}) async-start(bf16[64,2,640]{2,1,0:T(2,128)(2,1)} %reshape.499), calls=%async_computation.1 | async-start | bytes 327680 | tf_op jit(solution)/shard_map/all_to_all | solution.py:61
  314.9 5.0 %reshape.498 = bf16[512,2,8,10]{3,2,1,0:T(8,128)(2,1)S(1)} reshape(bf16[64,2,640]{2,1,0:T(2,128)(2,1)S(1)} %all-to-all-done.2) | data formatting | bytes 327680
  319.8 2.7 copy.70
  322.5 4.7 all_to_all.70
  327.3 7.1 %while.31 = (s32[]{:T(128)}, f32[8,8,1280]{2,1,0:T(8,128)S(1)}, bf16[8,8,2,640]{3,1,2,0:T(8,128)(2,1)}, f32[8,8,640]{2,1,0:T(8,128)S(1)}, f32[8,8,640]{2,1,0:T(8,128)S(1)}, /*index=5*/s32[]{:T(128)}) while((s32[]{:T(128)}, f32[8,8,1280]{2,1,0:T(8,128)S(1)}, bf16[8,8,2,640]{3,1,2,0:T(8,128)(2,1)}, f32[8,8,640]{2,1,0:T(8,128)S(1)}, ...), condition=%wide.region_11.13_spmd, body=%wide.region_8.12_spmd.sunk | while | flops 337922 | bytes 593997 | solution.py:34
  334.5 2.4 fusion.10
  336.8 10.9 %all-to-all-start.3 = ((bf16[64,2,640]{2,1,0:T(2,128)(2,1)}), bf16[64,2,640]{2,1,0:T(2,128)(2,1)}, u32[]{:S(2)}, u32[]{:S(2)}) async-start(bf16[64,2,640]{2,1,0:T(2,128)(2,1)} %reshape.495), calls=%async_computation.5 | async-start | bytes 327680 | tf_op jit(solution)/shard_map/all_to_all | solution.py:61
  348.0 6.0 %reshape.500 = bf16[512,2,8,10]{3,2,1,0:T(8,128)(2,1)} reshape(bf16[64,2,640]{2,1,0:T(2,128)(2,1)S(1)} %all-to-all-done.1) | data formatting | bytes 327680
  354.0 4.2 copy.63
  358.3 4.0 all_to_all.66
  362.3 1.5 while.30
  363.8 6.5 %reshape.496 = bf16[512,2,8,10]{3,2,1,0:T(8,128)(2,1)} reshape(bf16[64,2,640]{2,1,0:T(2,128)(2,1)} %all-to-all-done.3) | data formatting | bytes 327680
  370.2 4.2 copy.75
  374.5 4.0 all_to_all.74
  378.4 2.3 fusion.11
  380.9 1.5 while.32
  382.3 2.3 fusion.9
  384.7 13.1 %reduce-scatter.6.cloned.1.call-done = f32[2,8,512]{2,1,0:T(8,128)} async-done(((f32[8,8,512]{2,1,0:T(8,128)}), f32[2,8,512]{2,1,0:T(8,128)}) %reduce-scatter.6.cloned.1.call-update) | async-done | bytes 32784 | tf_op jit(solution)/shard_map/reduce_scatter | solution.py:74
  397.8 0.8 fusion.21
  398.6 43.6 %reduce-scatter.4.cloned.1.call-done = f32[2,8,512]{2,1,0:T(8,128)} async-done(((f32[8,8,512]{2,1,0:T(8,128)}), f32[2,8,512]{2,1,0:T(8,128)}) %reduce-scatter.4.cloned.1.call-update) | async-done | bytes 32784 | tf_op jit(solution)/shard_map/reduce_scatter | solution.py:74
  443.1 32.9 %reduce-scatter.8.cloned.1.call-done = f32[2,8,512]{2,1,0:T(8,128)} async-done(((f32[8,8,512]{2,1,0:T(8,128)}), f32[2,8,512]{2,1,0:T(8,128)}) %reduce-scatter.8.cloned.1.call-update) | async-done | bytes 32784 | tf_op jit(solution)/shard_map/reduce_scatter | solution.py:74
  (172 shorter events, 20.9 us)
Async XLA Ops:
  11.5 17.0 %copy-start.5 = (s32[3,64]{1,0:T(4,128)S(1)}, s32[3,64]{1,0:T(4,128)}, u32[]{:S(2)}) copy-start(s32[3,64]{1,0:T(4,128)} %param.12) | copy-start | bytes 2308
  11.5 24.6 %copy-start.4 = (bf16[8,8,2,640]{3,2,1,0:T(2,128)(2,1)S(1)}, bf16[8,8,2,640]{3,2,1,0:T(2,128)(2,1)}, u32[]{:S(2)}) copy-start(bf16[8,8,2,640]{3,2,1,0:T(2,128)(2,1)} %param.11) | copy-start | bytes 491524
  11.5 24.9 %copy-start.6 = (s32[512]{0:T(512)S(1)}, s32[512]{0:T(512)}, u32[]{:S(2)}) copy-start(s32[512]{0:T(512)} %param.13) | copy-start | bytes 6148
  11.6 37.6 %copy-start.7 = (u32[256]{0:T(256)S(1)}, u32[256]{0:T(256)}, u32[]{:S(2)}) copy-start(u32[256]{0:T(256)} %constant.173) | copy-start | bytes 3076
  15.0 176.2 %all-to-all-start = ((bf16[64,2,640]{2,1,0:T(2,128)(2,1)}), bf16[64,2,640]{2,1,0:T(2,128)(2,1)S(1)}, u32[]{:S(2)}, u32[]{:S(2)}) async-start(bf16[64,2,640]{2,1,0:T(2,128)(2,1)} %reshape.493), calls=%async_computation | async-start | bytes 327680 | tf_op jit(solution)/shard_map/all_to_all | solution.py:56
  235.6 10.2 %copy-start.3 = (bf16[64,8,8,2,10]{4,2,3,1,0:T(8,128)(2,1)S(1)}, bf16[64,8,8,2,10]{4,2,3,1,0:T(8,128)(2,1)}, u32[]{:S(2)}) copy-start(bf16[64,8,8,2,10]{4,2,3,1,0:T(8,128)(2,1)} %gather_fusion) | copy-start | bytes 491524
  240.7 63.1 %all-to-all-start.2 = ((bf16[64,2,640]{2,1,0:T(2,128)(2,1)}), bf16[64,2,640]{2,1,0:T(2,128)(2,1)S(1)}, u32[]{:S(2)}, u32[]{:S(2)}) async-start(bf16[64,2,640]{2,1,0:T(2,128)(2,1)} %reshape.497), calls=%async_computation.3 | async-start | bytes 327680 | tf_op jit(solution)/shard_map/all_to_all | solution.py:61
  270.4 5.1 %copy-start.2 = (bf16[64,8,8,2,10]{4,2,3,1,0:T(8,128)(2,1)S(1)}, bf16[64,8,8,2,10]{4,2,3,1,0:T(8,128)(2,1)}, u32[]{:S(2)}) copy-start(bf16[64,8,8,2,10]{4,2,3,1,0:T(8,128)(2,1)} %gather_fusion.6) | copy-start | bytes 491524
  303.8 33.0 %all-to-all-start.1 = ((bf16[64,2,640]{2,1,0:T(2,128)(2,1)}), bf16[64,2,640]{2,1,0:T(2,128)(2,1)S(1)}, u32[]{:S(2)}, u32[]{:S(2)}) async-start(bf16[64,2,640]{2,1,0:T(2,128)(2,1)} %reshape.499), calls=%async_computation.1 | async-start | bytes 327680 | tf_op jit(solution)/shard_map/all_to_all | solution.py:61
  314.6 83.2 %reduce-scatter.6.cloned.1.call-start = ((), (), s32[]{:S(2)}) async-start(), calls=%async_computation.8 | async-start | bytes 163840 | tf_op jit(solution)/shard_map/reduce_scatter | solution.py:74
  322.5 11.9 %copy-start = (f32[640,512]{1,0:T(8,128)S(1)}, f32[640,512]{1,0:T(8,128)}, u32[]{:S(2)}) copy-start(f32[640,512]{1,0:T(8,128)} %get-tuple-element.139) | copy-start | bytes 3932164
  322.5 11.9 %copy-start.1 = (f32[640,512]{1,0:T(8,128)S(1)}, f32[640,512]{1,0:T(8,128)}, u32[]{:S(2)}) copy-start(f32[640,512]{1,0:T(8,128)} %get-tuple-element.140) | copy-start | bytes 3932164
  336.8 26.9 %all-to-all-start.3 = ((bf16[64,2,640]{2,1,0:T(2,128)(2,1)}), bf16[64,2,640]{2,1,0:T(2,128)(2,1)}, u32[]{:S(2)}, u32[]{:S(2)}) async-start(bf16[64,2,640]{2,1,0:T(2,128)(2,1)} %reshape.495), calls=%async_computation.5 | async-start | bytes 327680 | tf_op jit(solution)/shard_map/all_to_all | solution.py:61
  347.7 94.5 %reduce-scatter.4.cloned.1.call-start = ((), (), s32[]{:S(2)}) async-start(), calls=%async_computation.7 | async-start | bytes 163840 | tf_op jit(solution)/shard_map/reduce_scatter | solution.py:74
  380.8 95.2 %reduce-scatter.8.cloned.1.call-start = ((), (), s32[]{:S(2)}) async-start(), calls=%async_computation.9 | async-start | bytes 163840 | tf_op jit(solution)/shard_map/reduce_scatter | solution.py:74
Sparse Core Ops, SparseCore 0:
  337.0 60.7 reduce-scatter.5
  400.6 41.5 reduce-scatter.3
  444.9 31.0 reduce-scatter.7
where the time goes:
time: 490 us; the launch traced here: 484 us
  local copies, waits for them, and re-layouts  165 us (34%)
  blocking collectives  139 us (28%)
  waiting for transfers between devices  89.7 us (18%)
  starting transfers between devices  40.8 us (8%)
  between operations  22 us (4%)
  other arithmetic  19.7 us (4%)
  matrix products  7.01 us (1%)
    unnamed x1, blocking collectives  131 us
    reduce_scatter x3, waiting for transfers between devices, per_device(): lax.psum_scatter(product.reshape(rows_kept * lax.axis_size('day'), own_ro...  89.6 us
    unnamed x28, local copies, waits for them, and re-layouts  45.3 us
    gather x9, local copies, waits for them, and re-layouts, per_device(): jnp.take_along_axis(picked, reorder[:, :, None, None, None], axis=1)  44.7 us
    all_to_all x3, starting transfers between devices, per_device(): lax.all_to_all(picked.reshape(blocks * own_rows, seg_dev, 2, -1), 'sta',...  26.7 us
    reshape x3, local copies, waits for them, and re-layouts, per_device(): picked.reshape(blocks * own_rows, seg_dev, 2, -1)  25.3 us
    all_to_all x6, local copies, waits for them, and re-layouts, per_device(): lax.all_to_all(picked.reshape(blocks * own_rows, seg_dev, 2, -1), 'sta',...  23.8 us
    all_to_all x1, starting transfers between devices, per_device(): lax.all_to_all(spectra, 'sta', split_axis=3, concat_axis=0, tiled=True)  13.5 us
  transfers between devices with their start and end apart: 7, of which 3 were waited for; matrix products, arithmetic and copies ran while one was open for 25% of the time, Pallas kernels for 0%

commit v1 on v0

v1 whole, which is shorter than its diff:
```python
import functools

import jax
import jax.numpy as jnp
import ml_dtypes
import numpy as np
from jax import lax
from jax.experimental import pallas as pl
from jax.experimental.pallas import tpu as pltpu
from jax.sharding import PartitionSpec as P

BIN_LO = 60
SEGLEN = 6000
LAGS = 512
ROUNDS = 3
EPS = 1e-06
NFREQ = 640
SPB = 8
SEG = 8
DAYS = 4
BLOCKS = 64
BANDS = 40
ROWS = 16
LANES = 128
TILES = NFREQ // LANES
LAG_TILES = LAGS // LANES
PARTS = 2 * LAG_TILES + 3
MESH = pl.DeviceIdType.MESH


def lag_table():
    bins = BIN_LO + np.arange(NFREQ, dtype=np.int64)
    shifts = np.arange(LAGS, dtype=np.int64) - LAGS // 2
    turns = np.mod(bins[:, None] * shifts[None, :], SEGLEN)
    angle = 2.0 * np.pi / SEGLEN * turns
    table = np.concatenate([np.cos(angle), -np.sin(angle)], axis=0).astype(np.float32)
    high = table.astype(ml_dtypes.bfloat16)
    low = (table - high.astype(np.float32)).astype(ml_dtypes.bfloat16)
    return np.stack([high, low])


def band_place(band):
    z, turn = band // 5, band % 5
    return z * 8 + (turn + 3 * z) % 8


def kernel(
    x_ref, pairing_ref, slot_ref, table_hbm, out_ref,
    natural, own, sent, banded, picked, returned, partner, cross, sums, met, table,
    table_sem, first_send, first_recv, back_send, back_recv, day_send, day_recv,
):
    sta, day = lax.axis_index("sta"), lax.axis_index("day")
    plane = sta // 8
    turn = (sta % 8 + 5 * plane) % 8
    is_band = turn < 5
    band = plane * 5 + turn

    barrier = pltpu.get_barrier_semaphore()

    def greet(k, carry):
        pl.semaphore_signal(
            barrier, inc=1, device_id=((sta + k) % BLOCKS, day), device_id_type=MESH
        )
        return carry

    lax.fori_loop(1, BLOCKS, greet, 0, unroll=7)
    for k in range(1, DAYS):
        pl.semaphore_signal(
            barrier, inc=1, device_id=(sta, (day + k) % DAYS), device_id_type=MESH
        )
    load_table = pltpu.make_async_copy(table_hbm, table, table_sem)
    load_table.start()

    for c in range(2):
        part = x_ref[:, c, :].astype(jnp.float32)
        natural[c] = part.reshape(SPB, SEG, NFREQ)
    slots = [slot_ref[sta * SPB + i] for i in range(SPB)]
    order = []
    for j in range(SPB):
        at = jnp.int32(0)
        for i in range(1, SPB):
            at = jnp.where(slots[i] == j, i, at)
        order.append(at)
    rows = jnp.concatenate(
        [natural[c, order[j]] for c in range(2) for j in range(SPB)], axis=0
    )
    for t in range(TILES):
        tile = rows[:, t * LANES : (t + 1) * LANES].T.astype(jnp.bfloat16)
        sent[t * 8 : (t + 1) * 8] = tile.reshape(8, ROWS, LANES)

    pl.semaphore_wait(barrier, BLOCKS - 1 + DAYS - 1)

    def first(k):
        to = (sta + k) % BANDS
        place = band_place(to)
        return place, pltpu.make_async_remote_copy(
            src_ref=sent.at[to], dst_ref=banded.at[sta], send_sem=first_send, recv_sem=first_recv,
            device_id=(place, day), device_id_type=MESH,
        )

    def send_first(k, carry):
        place, copy = first(k)

        @pl.when(place != sta)
        def _():
            copy.start()

        return carry

    lax.fori_loop(0, BANDS, send_first, 0, unroll=4)

    @pl.when(is_band)
    def _():
        pltpu.make_async_copy(sent.at[band], banded.at[sta], first_recv).start()

    for seg in range(SEG):
        for c in range(2):
            own[c, seg] = natural[c, :, seg, :]
    own_energy = jnp.zeros((SPB, LANES), jnp.float32)
    for c in range(2):
        for seg in range(SEG):
            square = own[c, seg] * own[c, seg]
            for t in range(TILES):
                own_energy = own_energy + square[:, t * LANES : (t + 1) * LANES]

    @pl.when(is_band)
    def _():
        pltpu.make_async_copy(banded, banded, first_recv).wait()
        for r in range(ROUNDS):

            def pick(b, carry):
                picked[r, b] = banded[pairing_ref[r, b]]
                return carry

            lax.fori_loop(0, BLOCKS, pick, 0, unroll=8)

            def send_back(k, carry):
                to = (sta + k) % BLOCKS
                pltpu.make_async_remote_copy(
                    src_ref=picked.at[r, to], dst_ref=returned.at[r, band],
                    send_sem=back_send, recv_sem=back_recv.at[r],
                    device_id=(to, day), device_id_type=MESH,
                ).start()
                return carry

            pltpu.make_async_copy(
                picked.at[r, sta], returned.at[r, band], back_recv.at[r]
            ).start()
            lax.fori_loop(1, BLOCKS, send_back, 0, unroll=7)

    load_table.wait()
    for r in range(ROUNDS):
        pltpu.make_async_copy(returned.at[r], returned.at[r], back_recv.at[r]).wait()
        for t in range(TILES):
            tile = returned[r, t * 8 : (t + 1) * 8].reshape(LANES, LANES)
            tile = tile.astype(jnp.float32).T
            partner[:, :, :, t * LANES : (t + 1) * LANES] = tile.reshape(2, SPB, SEG, LANES)

        def correlate(j, carry):
            real = jnp.zeros((SPB, NFREQ), jnp.float32)
            imag = jnp.zeros((SPB, NFREQ), jnp.float32)
            for seg in range(SEG):
                x_re, x_im = own[0, seg], own[1, seg]
                y_re = partner[0, j, seg : seg + 1, :]
                y_im = partner[1, j, seg : seg + 1, :]
                real = real + x_re * y_re + x_im * y_im
                imag = imag + x_im * y_re - x_re * y_im
            cross[j, :, :NFREQ] = real
            cross[j, :, NFREQ:] = imag
            return carry

        lax.fori_loop(0, SPB, correlate, 0)
        spectrum = cross[...].reshape(SPB * SPB, 2 * NFREQ)
        high = spectrum.astype(jnp.bfloat16)
        low = (spectrum - high.astype(jnp.float32)).astype(jnp.bfloat16)
        dot = functools.partial(jnp.dot, preferred_element_type=jnp.float32)
        raw = dot(high, table[0]) + dot(low, table[0]) + dot(high, table[1])
        for j in range(SPB):
            to, at = j // 2, j % 2
            for t in range(LAG_TILES):
                sums[r, to, at * LAG_TILES + t] = raw[
                    j * SPB : (j + 1) * SPB, t * LANES : (t + 1) * LANES
                ]
            energy = jnp.zeros((SEG, LANES), jnp.float32)
            for c in range(2):
                for t in range(TILES):
                    y = partner[c, j, :, t * LANES : (t + 1) * LANES]
                    energy = energy + y * y
            sums[r, to, 2 * LAG_TILES + 1 + at] = energy
        for to in range(DAYS):
            sums[r, to, 2 * LAG_TILES] = own_energy
        for k in range(1, DAYS):
            to = (day + k) % DAYS
            pltpu.make_async_remote_copy(
                src_ref=sums.at[r, to], dst_ref=met.at[r, day], send_sem=day_send, recv_sem=day_recv.at[r],
                device_id=(sta, to), device_id_type=MESH,
            ).start()
        pltpu.make_async_copy(sums.at[r, day], met.at[r, day], day_recv.at[r]).start()

    for r in range(ROUNDS):
        pltpu.make_async_copy(met.at[r], met.at[r], day_recv.at[r]).wait()
        total = met[r, 0] + met[r, 1] + met[r, 2] + met[r, 3]
        count = float(SEG * DAYS * 2 * NFREQ)
        energy_i = jnp.sum(total[2 * LAG_TILES], axis=1, keepdims=True) / count + EPS
        for at in range(2):
            energy_j = jnp.sum(total[2 * LAG_TILES + 1 + at], axis=1, keepdims=True)
            energy_j = jnp.sum(energy_j, axis=0, keepdims=True) / count + EPS
            scale = 1.0 / (jnp.sqrt(energy_j * energy_i) * np.float32(np.sqrt(count)))
            for t in range(LAG_TILES):
                out_ref[r, at, :, t * LANES : (t + 1) * LANES] = (
                    total[at * LAG_TILES + t] * scale
                ).astype(jnp.bfloat16)

    @pl.when(is_band)
    def _():
        pltpu.make_async_copy(
            sent.at[pl.ds(0, BANDS - 1)], sent.at[pl.ds(0, BANDS - 1)], first_send
        ).wait()
        for r in range(ROUNDS):
            pltpu.make_async_copy(
                picked.at[r, pl.ds(0, BLOCKS - 1)], picked.at[r, pl.ds(0, BLOCKS - 1)], back_send
            ).wait()

    @pl.when(jnp.logical_not(is_band))
    def _():
        pltpu.make_async_copy(sent, sent, first_send).wait()

    for r in range(ROUNDS):
        pltpu.make_async_copy(
            sums.at[r, pl.ds(0, DAYS - 1)], sums.at[r, pl.ds(0, DAYS - 1)], day_send
        ).wait()


def per_device(spectra, pairing, station_slot):
    x = spectra.reshape(SPB * SEG, 2, NFREQ)
    vmem = pl.BlockSpec(memory_space=pltpu.VMEM)
    smem = pl.BlockSpec(memory_space=pltpu.SMEM)
    dma = pltpu.SemaphoreType.DMA
    f32, bf16 = jnp.float32, jnp.bfloat16
    return pl.pallas_call(
        kernel,
        out_shape=jax.ShapeDtypeStruct((ROUNDS, 2, SPB, LAGS), bf16),
        in_specs=[vmem, smem, smem, pl.BlockSpec(memory_space=pl.ANY)],
        out_specs=vmem,
        scratch_shapes=[
            pltpu.VMEM((2, SPB, SEG, NFREQ), f32),
            pltpu.VMEM((2, SEG, SPB, NFREQ), f32),
            pltpu.VMEM((BANDS, ROWS, LANES), bf16),
            pltpu.VMEM((BLOCKS, ROWS, LANES), bf16),
            pltpu.VMEM((ROUNDS, BLOCKS, ROWS, LANES), bf16),
            pltpu.VMEM((ROUNDS, BANDS, ROWS, LANES), bf16),
            pltpu.VMEM((2, SPB, SEG, NFREQ), f32),
            pltpu.VMEM((SPB, SPB, 2 * NFREQ), f32),
            pltpu.VMEM((ROUNDS, DAYS, PARTS, SPB, LANES), f32),
            pltpu.VMEM((ROUNDS, DAYS, PARTS, SPB, LANES), f32),
            pltpu.VMEM((2, 2 * NFREQ, LAGS), bf16),
            dma, dma, dma, dma, dma((ROUNDS,)), dma, dma((ROUNDS,)),
        ],
        compiler_params=pltpu.CompilerParams(
            collective_id=0, has_side_effects=True, vmem_limit_bytes=48 * 1024 * 1024
        ),
        name="correlate",
    )(x, pairing, station_slot, jnp.asarray(lag_table()))


def solution(mesh):
    in_specs = (P("sta", "day", None, None), P(), P())
    out_specs = P(None, "day", "sta", None)
    return jax.shard_map(
        per_device, mesh=mesh, in_specs=in_specs, out_specs=out_specs, check_vma=False
    )
```

time: 490 us -> 49 us (0.10); the launches traced: 484 us -> 48.8 us
  local copies, waits for them, and re-layouts: 165 us -> 4.64 us
  blocking collectives: 139 us -> 0 us
  waiting for transfers between devices: 89.7 us -> 0 us
  Pallas kernels: 0 us -> 44.1 us
  starting transfers between devices: 40.8 us -> 0 us
  between operations: 22 us -> 0.01 us
  other arithmetic: 19.7 us -> 0 us
  matrix products: 7.01 us -> 0 us
    unnamed x1 -> x0, blocking collectives: 131 us -> none
    reduce_scatter x3 -> x0, waiting for transfers between devices: 89.6 us -> none  [per_device(): lax.psum_scatter(product.reshape(rows_kept * lax.axis_size('day'), own_ro...]
    gather x18 -> x0, local copies, waits for them, and re-layouts: 54.9 us -> none  [the longest x9 44.7 us: per_device(): jnp.take_along_axis(picked, reorder[:, :, None, None, None], axis=1)]
    pallas_call x0 -> x1, Pallas kernels: none -> 44.1 us  [per_device(): pl.pallas_call(kernel, out_shape=jax.ShapeDtypeStruct((ROUNDS, 2, SPB, LA...]
    unnamed x28 -> x9, local copies, waits for them, and re-layouts: 45.3 us -> 4.64 us
    all_to_all x4 -> x0, starting transfers between devices: 40.2 us -> none  [the longest x3 26.7 us: per_device(): lax.all_to_all(picked.reshape(blocks * own_rows, seg_dev, 2, -1), 'sta',...]
    all_to_all x7 -> x0, local copies, waits for them, and re-layouts: 31.2 us -> none  [the longest x6 23.8 us: per_device(): lax.all_to_all(picked.reshape(blocks * own_rows, seg_dev, 2, -1), 'sta',...]
    reshape x5 -> x0, local copies, waits for them, and re-layouts: 25.4 us -> none  [the longest x3 25.3 us: per_device(): picked.reshape(blocks * own_rows, seg_dev, 2, -1)]
  transfers between devices with their start and end apart: 7 -> 0, of which waited for: 3 -> 0; matrix products, arithmetic and copies ran while one was open for 25% -> 0% of each run, Pallas kernels for 0% -> 0%
where the time goes in v1:
time: 49 us; the launch traced here: 48.8 us
  Pallas kernels  44.1 us (90%)
  local copies, waits for them, and re-layouts  4.64 us (9%)
    pallas_call x1, Pallas kernels, per_device(): pl.pallas_call(kernel, out_shape=jax.ShapeDtypeStruct((ROUNDS, 2, SPB, LA...  44.1 us
    unnamed x9, local copies, waits for them, and re-layouts  4.64 us

profile of v1, /device:TPU:1, one launch (start us, length us, event | category | flops | bytes accessed | tf_op | source)
XLA Modules:
  0.0 48.8 jit_solution(17483861053866205653)
XLA Ops:
  0.0 0.0 copy-start
  0.0 1.7 %copy-done = bf16[2,1280,512]{2,1,0:T(8,128)(2,1)S(1)} copy-done((bf16[2,1280,512]{2,1,0:T(8,128)(2,1)S(1)}, bf16[2,1280,512]{2,1,0:T(8,128)(2,1)}, u32[]{:S(2)}) %copy-start) | copy-done | bytes 2621464
  1.7 0.0 copy-start.1
  1.7 0.9 %copy-done.1 = bf16[8,8,2,640]{3,2,1,0:T(2,128)(2,1)S(1)} copy-done((bf16[8,8,2,640]{3,2,1,0:T(2,128)(2,1)S(1)}, bf16[8,8,2,640]{3,2,1,0:T(2,128)(2,1)}, u32[]{:S(2)}) %copy-start.1) | copy-done | bytes 163864
  2.7 0.0 copy-start.2
  2.7 0.7 %copy-done.2 = s32[3,64]{1,0:T(4,128)S(1)} copy-done((s32[3,64]{1,0:T(4,128)S(1)}, s32[3,64]{1,0:T(4,128)}, u32[]{:S(2)}) %copy-start.2) | copy-done | bytes 792
  3.3 0.0 copy-start.3
  3.3 0.7 %copy-done.3 = s32[512]{0:T(512)S(1)} copy-done((s32[512]{0:T(512)S(1)}, s32[512]{0:T(512)}, u32[]{:S(2)}) %copy-start.3) | copy-done | bytes 2072
  4.0 44.1 %correlate.1 = bf16[3,2,8,512]{3,2,1,0:T(8,128)(2,1)S(1)} custom-call(bf16[64,2,640]{2,1,0:T(2,128)(2,1)S(1)} %bitcast.1, s32[3,64]{1,0:T(4,128)S(1)} %copy-done.2, s32[512]{0:T(512)S(1)} %copy-done.3, bf16[2,1280,512]{2,1,0:T(8,128)(2,1)S(1)} %copy-done), custom_call_target="tpu_custom_call" | custom-call | tf_op jit(solution)/shard_map/correlate/pallas_call | solution.py:240
  48.2 0.6 %copy.6 = bf16[3,2,8,512]{3,2,1,0:T(8,128)(2,1)} copy(bf16[3,2,8,512]{3,2,1,0:T(8,128)(2,1)S(1)} %correlate.1) | data formatting | bytes 98304
Async XLA Ops:
  0.0 1.7 %copy-start = (bf16[2,1280,512]{2,1,0:T(8,128)(2,1)S(1)}, bf16[2,1280,512]{2,1,0:T(8,128)(2,1)}, u32[]{:S(2)}) copy-start(bf16[2,1280,512]{2,1,0:T(8,128)(2,1)} %constant.2.clone.table_hbm) | copy-start | bytes 7864324
  1.7 0.9 %copy-start.1 = (bf16[8,8,2,640]{3,2,1,0:T(2,128)(2,1)S(1)}, bf16[8,8,2,640]{3,2,1,0:T(2,128)(2,1)}, u32[]{:S(2)}) copy-start(bf16[8,8,2,640]{3,2,1,0:T(2,128)(2,1)} %param.4) | copy-start | bytes 491524
  2.7 0.7 %copy-start.2 = (s32[3,64]{1,0:T(4,128)S(1)}, s32[3,64]{1,0:T(4,128)}, u32[]{:S(2)}) copy-start(s32[3,64]{1,0:T(4,128)} %pairing_ref.1) | copy-start | bytes 2308
  3.3 0.7 %copy-start.3 = (s32[512]{0:T(512)S(1)}, s32[512]{0:T(512)}, u32[]{:S(2)}) copy-start(s32[512]{0:T(512)} %slot_ref.1) | copy-start | bytes 6148

commit v2 on v1

v2 whole, which is shorter than its diff:
```python
import functools

import jax
import jax.numpy as jnp
import ml_dtypes
import numpy as np
from jax import lax
from jax.experimental import pallas as pl
from jax.experimental.pallas import tpu as pltpu
from jax.sharding import PartitionSpec as P

BIN_LO = 60
SEGLEN = 6000
LAGS = 512
ROUNDS = 3
EPS = 1e-06
NFREQ = 640
SPB = 8
SEG = 8
DAYS = 4
BLOCKS = 64
BANDS = 10
KEPT = BANDS * DAYS
ROWS = 16
LANES = 128
PIECE = 32
TILES = NFREQ // LANES
WHOLE = 512
MESH = pl.DeviceIdType.MESH


def lag_table():
    bins = BIN_LO + np.arange(NFREQ, dtype=np.int64)
    shifts = np.arange(LAGS, dtype=np.int64) - LAGS // 2
    turns = np.mod(bins[:, None] * shifts[None, :], SEGLEN)
    angle = 2.0 * np.pi / SEGLEN * turns
    table = np.concatenate([np.cos(angle), -np.sin(angle)], axis=0).astype(np.float32)
    high = table.astype(ml_dtypes.bfloat16)
    low = (table - high.astype(np.float32)).astype(ml_dtypes.bfloat16)
    return np.stack([high, low])


def keeper(kept, core):
    z, turn = kept // 5, kept % 5
    return z * 8 + (turn + 3 * core + 2 * z) % 8


def kernel(
    x_hbm, pairing_hbm, slot_hbm, table_hbm, out_ref,
    spectra, pairing_ref, slot_ref, natural, own, sent, banded, picked, returned, partner, cross, table,
    load_sem, first_send, first_recv, back_send, back_recv, own_send, own_recv,
):
    sta, day = lax.axis_index("sta"), lax.axis_index("day")
    plane = sta // 8
    turn = (sta % 8 + 6 * plane + 5 * (day % 2)) % 8
    is_keeper = turn < 5
    kept = plane * 5 + turn
    band, origin = kept // DAYS, kept % DAYS
    keeps_own = jnp.logical_and(is_keeper, origin == day)

    loads = [
        pltpu.make_async_copy(source, target, load_sem.at[i])
        for i, (source, target) in enumerate(
            [(x_hbm, spectra.at[day]), (slot_hbm, slot_ref), (pairing_hbm, pairing_ref), (table_hbm, table)]
        )
    ]
    for load in loads:
        load.start()

    barrier = pltpu.get_barrier_semaphore()

    def greet(place, to_day):
        pl.semaphore_signal(barrier, inc=1, device_id=(place, to_day), device_id_type=MESH)

    @pl.when(is_keeper)
    def _():
        def greet_block(k, carry):
            greet((sta + k) % BLOCKS, origin)
            return carry

        lax.fori_loop(1, BLOCKS, greet_block, 0, unroll=7)

        @pl.when(origin != day)
        def _():
            greet(sta, origin)

    def greet_keeper(k, carry):
        place = keeper((sta + k) % KEPT, day % 2)

        @pl.when(place != sta)
        def _():
            greet(place, day)

        return carry

    lax.fori_loop(0, KEPT, greet_keeper, 0, unroll=4)
    for k in range(1, DAYS):
        greet(sta, (day + k) % DAYS)

    for load in loads[:2]:
        load.wait()

    def split(day_from):
        for c in range(2):
            part = spectra[day_from, :, c, :].astype(jnp.float32)
            natural[c] = part.reshape(SPB, SEG, NFREQ)

    split(day)
    slots = [slot_ref[sta * SPB + i] for i in range(SPB)]
    order = []
    for j in range(SPB):
        at = jnp.int32(0)
        for i in range(1, SPB):
            at = jnp.where(slots[i] == j, i, at)
        order.append(at)
    pairs = [
        jnp.concatenate(
            [natural[c, order[2 * to + j]] for c in range(2) for j in range(2)], axis=0
        )
        for to in range(DAYS)
    ]
    quarter = lax.broadcasted_iota(jnp.int32, (PIECE, LANES), 1) // PIECE
    for to in range(DAYS):
        tile = jnp.concatenate(
            [pairs[to][:, g * LANES : (g + 1) * LANES] for g in range(4)], axis=0
        )
        sent[to * BANDS : to * BANDS + 8] = tile.T.astype(jnp.bfloat16).reshape(8, ROWS, LANES)
    rest = []
    for g in range(4):
        piece = jnp.zeros((PIECE, LANES), jnp.float32)
        for to in range(DAYS):
            moved = pairs[to][:, WHOLE:]
            if to != g:
                moved = pltpu.roll(moved, (PIECE * (to - g)) % LANES, 1)
            piece = jnp.where(quarter == to, moved, piece)
        rest.append(piece)
    rest = jnp.concatenate(rest, axis=0).T.astype(jnp.bfloat16)
    for to in range(DAYS):
        sent[to * BANDS + 8 : (to + 1) * BANDS] = rest[to * PIECE : (to + 1) * PIECE].reshape(
            2, ROWS, LANES
        )

    loads[2].wait()
    greetings = KEPT + DAYS - 1 + jnp.where(is_keeper, BLOCKS - 1, 0) - jnp.where(keeps_own, 1, 0)
    pl.semaphore_wait(barrier, greetings)

    def send_first(k, carry):
        at = (sta + k) % KEPT
        to = at // BANDS
        place = keeper(at % BANDS * DAYS + day, to % 2)

        @pl.when(jnp.logical_or(place != sta, to != day))
        def _():
            pltpu.make_async_remote_copy(
                src_ref=sent.at[at], dst_ref=banded.at[sta], send_sem=first_send, recv_sem=first_recv,
                device_id=(place, to), device_id_type=MESH,
            ).start()

        return carry

    lax.fori_loop(0, KEPT, send_first, 0, unroll=4)

    @pl.when(keeps_own)
    def _():
        pltpu.make_async_copy(sent.at[day * BANDS + band], banded.at[sta], first_recv).start()

    for k in range(1, DAYS):
        pltpu.make_async_remote_copy(
            src_ref=spectra.at[day], dst_ref=spectra.at[day], send_sem=own_send, recv_sem=own_recv.at[k - 1],
            device_id=(sta, (day + k) % DAYS), device_id_type=MESH,
        ).start()

    @pl.when(is_keeper)
    def _():
        pltpu.make_async_copy(banded, banded, first_recv).wait()
        for r in range(ROUNDS):

            def pick(b, carry):
                picked[r, b] = banded[pairing_ref[r, b]]
                return carry

            lax.fori_loop(0, BLOCKS, pick, 0, unroll=8)

            def send_back(k, carry):
                to = (sta + k) % BLOCKS
                pltpu.make_async_remote_copy(
                    src_ref=picked.at[r, to], dst_ref=returned.at[r, origin * BANDS + band],
                    send_sem=back_send, recv_sem=back_recv.at[r],
                    device_id=(to, day), device_id_type=MESH,
                ).start()
                return carry

            pltpu.make_async_copy(
                picked.at[r, sta], returned.at[r, origin * BANDS + band], back_recv.at[r]
            ).start()
            lax.fori_loop(1, BLOCKS, send_back, 0, unroll=7)

    for k in range(1, DAYS):
        pltpu.make_async_copy(spectra.at[0], spectra.at[0], own_recv.at[k - 1]).wait()
    square = jnp.zeros((SPB, LANES), jnp.float32)
    for q in range(DAYS):
        split(q)
        for c in range(2):
            for seg in range(SEG):
                x = natural[c, :, seg, :]
                own[c, q, seg] = x
                for t in range(TILES):
                    x_t = x[:, t * LANES : (t + 1) * LANES]
                    square = square + x_t * x_t
    count = float(SEG * DAYS * 2 * NFREQ)
    energy_i = jnp.sum(square, axis=1, keepdims=True) / count + EPS

    loads[3].wait()
    dot = functools.partial(jnp.dot, preferred_element_type=jnp.float32)
    for r in range(ROUNDS):
        pltpu.make_async_copy(returned.at[r], returned.at[r], back_recv.at[r]).wait()
        for q in range(DAYS):
            tile = returned[r, q * BANDS : q * BANDS + 8].reshape(LANES, LANES)
            tile = tile.astype(jnp.float32).T.reshape(4, 2, 2, SEG, LANES)
            for g in range(4):
                partner[:, :, q, :, g * LANES : (g + 1) * LANES] = tile[g]
        rest = jnp.concatenate(
            [
                returned[r, q * BANDS + 8 : (q + 1) * BANDS].reshape(PIECE, LANES)
                for q in range(DAYS)
            ],
            axis=0,
        )
        rest = rest.astype(jnp.float32).T
        for q in range(DAYS):
            piece = jnp.zeros((PIECE, LANES), jnp.float32)
            for g in range(4):
                moved = rest[g * PIECE : (g + 1) * PIECE]
                if g != q:
                    moved = pltpu.roll(moved, (PIECE * (g - q)) % LANES, 1)
                piece = jnp.where(quarter == g, moved, piece)
            partner[:, :, q, :, WHOLE:] = piece.reshape(2, 2, SEG, LANES)

        def correlate(q, sums):
            sums = list(sums)
            for seg in range(SEG):
                x_re, x_im = own[0, q, seg], own[1, q, seg]
                for j in range(2):
                    y_re = partner[0, j, q, seg : seg + 1, :]
                    y_im = partner[1, j, q, seg : seg + 1, :]
                    sums[2 * j] = sums[2 * j] + x_re * y_re + x_im * y_im
                    sums[2 * j + 1] = sums[2 * j + 1] + x_im * y_re - x_re * y_im
            return tuple(sums)

        zero = jnp.zeros((SPB, NFREQ), jnp.float32)
        sums = lax.fori_loop(0, DAYS, correlate, (zero,) * 4)
        for j in range(2):
            for c in range(2):
                cross[j * SPB : (j + 1) * SPB, c * NFREQ : (c + 1) * NFREQ] = sums[2 * j + c]
        spectrum = cross[...]
        high = spectrum.astype(jnp.bfloat16)
        low = (spectrum - high.astype(jnp.float32)).astype(jnp.bfloat16)
        raw = dot(high, table[0]) + dot(low, table[0]) + dot(high, table[1])
        for j in range(2):
            square = jnp.zeros((SEG, LANES), jnp.float32)
            for c in range(2):
                for q in range(DAYS):
                    for t in range(TILES):
                        y = partner[c, j, q, :, t * LANES : (t + 1) * LANES]
                        square = square + y * y
            energy_j = jnp.sum(square, axis=1, keepdims=True)
            energy_j = jnp.sum(energy_j, axis=0, keepdims=True) / count + EPS
            scale = 1.0 / (jnp.sqrt(energy_j * energy_i) * np.float32(np.sqrt(count)))
            out_ref[r, j] = (raw[j * SPB : (j + 1) * SPB] * scale).astype(jnp.bfloat16)

    @pl.when(keeps_own)
    def _():
        rest_sent = sent.at[pl.ds(0, KEPT - 1)]
        pltpu.make_async_copy(rest_sent, rest_sent, first_send).wait()

    @pl.when(jnp.logical_not(keeps_own))
    def _():
        pltpu.make_async_copy(sent, sent, first_send).wait()

    @pl.when(is_keeper)
    def _():
        for r in range(ROUNDS):
            rest_sent = picked.at[r, pl.ds(0, BLOCKS - 1)]
            pltpu.make_async_copy(rest_sent, rest_sent, back_send).wait()

    rest_sent = spectra.at[pl.ds(0, DAYS - 1)]
    pltpu.make_async_copy(rest_sent, rest_sent, own_send).wait()


def per_device(spectra, pairing, station_slot):
    x = spectra.reshape(SPB * SEG, 2, NFREQ)
    hbm = pl.BlockSpec(memory_space=pltpu.HBM)
    dma = pltpu.SemaphoreType.DMA
    f32, bf16 = jnp.float32, jnp.bfloat16
    return pl.pallas_call(
        kernel,
        out_shape=jax.ShapeDtypeStruct((ROUNDS, 2, SPB, LAGS), bf16),
        in_specs=[hbm] * 4,
        out_specs=pl.BlockSpec(memory_space=pltpu.VMEM),
        scratch_shapes=[
            pltpu.VMEM((DAYS,) + x.shape, bf16),
            pltpu.SMEM(pairing.shape, jnp.int32),
            pltpu.SMEM(station_slot.shape, jnp.int32),
            pltpu.VMEM((2, SPB, SEG, NFREQ), f32),
            pltpu.VMEM((2, DAYS, SEG, SPB, NFREQ), f32),
            pltpu.VMEM((KEPT, ROWS, LANES), bf16),
            pltpu.VMEM((BLOCKS, ROWS, LANES), bf16),
            pltpu.VMEM((ROUNDS, BLOCKS, ROWS, LANES), bf16),
            pltpu.VMEM((ROUNDS, KEPT, ROWS, LANES), bf16),
            pltpu.VMEM((2, 2, DAYS, SEG, NFREQ), f32),
            pltpu.VMEM((2 * SPB, 2 * NFREQ), f32),
            pltpu.VMEM((2, 2 * NFREQ, LAGS), bf16),
            dma((4,)), dma, dma, dma, dma((ROUNDS,)), dma, dma((DAYS - 1,)),
        ],
        compiler_params=pltpu.CompilerParams(
            collective_id=0, has_side_effects=True, vmem_limit_bytes=63 * 1024 * 1024
        ),
        name="correlate",
    )(x, pairing, station_slot, jnp.asarray(lag_table()))


def solution(mesh):
    in_specs = (P("sta", "day", None, None), P(), P())
    out_specs = P(None, "day", "sta", None)
    return jax.shard_map(
        per_device, mesh=mesh, in_specs=in_specs, out_specs=out_specs, check_vma=False
    )
```

time: 49 us -> 41.4 us (0.84)
  Pallas kernels: 44.1 us -> 39.8 us
  local copies, waits for them, and re-layouts: 4.64 us -> 1.42 us
    pallas_call x1, Pallas kernels: 44.1 us -> 39.8 us  [per_device(): pl.pallas_call(kernel, out_shape=jax.ShapeDtypeStruct((ROUNDS, 2, SPB, LA...]
    unnamed x9 -> x1, local copies, waits for them, and re-layouts: 4.64 us -> 1.42 us
where the time goes in v2:
time: 41.4 us; the launch traced here: 41.2 us
  Pallas kernels  39.8 us (96%)
  local copies, waits for them, and re-layouts  1.42 us (3%)
    pallas_call x1, Pallas kernels, per_device(): pl.pallas_call(kernel, out_shape=jax.ShapeDtypeStruct((ROUNDS, 2, SPB, LA...  39.8 us
    unnamed x1, local copies, waits for them, and re-layouts  1.42 us

profile of v2, /device:TPU:1, one launch (start us, length us, event | category | flops | bytes accessed | tf_op | source)
XLA Modules:
  0.0 41.2 jit_solution(2698143701187038826)
XLA Ops:
  0.0 39.8 %correlate.1 = bf16[3,2,8,512]{3,2,1,0:T(8,128)(2,1)} custom-call(bf16[64,2,640]{2,1,0:T(2,128)(2,1)} %bitcast.1, s32[3,64]{1,0:T(4,128)} %pairing_hbm.1, s32[512]{0:T(512)} %slot_hbm.1, bf16[2,1280,512]{2,1,0:T(8,128)(2,1)} %constant.2.clone.table_hbm), custom_call_target="tpu_custom_call" | custom-call | tf_op jit(solution)/shard_map/correlate/pallas_call | solution.py:295
  39.8 1.4 %copy.6 = bf16[3,2,8,512]{3,2,1,0:T(8,128)(2,1)} copy(bf16[3,2,8,512]{3,2,1,0:T(8,128)(2,1)} %correlate.1) | data formatting | bytes 98304

commit v3 on v2

--- a/solution.py
+++ b/solution.py
@@ -45,6 +45,15 @@
     return z * 8 + (turn + 3 * core + 2 * z) % 8
 
 
+def outward(k, half):
+    return half + (k + 1) // 2 * (1 - 2 * (k % 2))
+
+
+def far_first(sta, k):
+    plane = (sta // 8 + outward(k // 8, 4)) % 8
+    return plane * 8 + (sta % 8 + k % 8 + 1) % 8
+
+
 def kernel(
     x_hbm, pairing_hbm, slot_hbm, table_hbm, out_ref,
     spectra, pairing_ref, slot_ref, natural, own, sent, banded, picked, returned, partner, cross, table,
@@ -58,6 +67,26 @@
     band, origin = kept // DAYS, kept % DAYS
     keeps_own = jnp.logical_and(is_keeper, origin == day)
 
+    barrier = pltpu.get_barrier_semaphore()
+
+    def greet(place, to_day):
+        pl.semaphore_signal(barrier, inc=1, device_id=(place, to_day), device_id_type=MESH)
+
+    @pl.when(is_keeper)
+    def _():
+        def greet_block(k, carry):
+            greet(far_first(sta, k), origin)
+            return carry
+
+        lax.fori_loop(0, BLOCKS - 1, greet_block, 0, unroll=7)
+
+        @pl.when(origin != day)
+        def _():
+            greet(sta, origin)
+
+    for k in range(1, DAYS):
+        greet(sta, (day + k) % DAYS)
+
     loads = [
         pltpu.make_async_copy(source, target, load_sem.at[i])
         for i, (source, target) in enumerate(
@@ -66,36 +95,6 @@
     ]
     for load in loads:
         load.start()
-
-    barrier = pltpu.get_barrier_semaphore()
-
-    def greet(place, to_day):
-        pl.semaphore_signal(barrier, inc=1, device_id=(place, to_day), device_id_type=MESH)
-
-    @pl.when(is_keeper)
-    def _():
-        def greet_block(k, carry):
-            greet((sta + k) % BLOCKS, origin)
-            return carry
-
-        lax.fori_loop(1, BLOCKS, greet_block, 0, unroll=7)
-
-        @pl.when(origin != day)
-        def _():
-            greet(sta, origin)
-
-    def greet_keeper(k, carry):
-        place = keeper((sta + k) % KEPT, day % 2)
-
-        @pl.when(place != sta)
-        def _():
-            greet(place, day)
-
-        return carry
-
-    lax.fori_loop(0, KEPT, greet_keeper, 0, unroll=4)
-    for k in range(1, DAYS):
-        greet(sta, (day + k) % DAYS)
 
     for load in loads[:2]:
         load.wait()
@@ -141,13 +140,14 @@
         )
 
     loads[2].wait()
-    greetings = KEPT + DAYS - 1 + jnp.where(is_keeper, BLOCKS - 1, 0) - jnp.where(keeps_own, 1, 0)
+    greetings = KEPT + DAYS - 1 - jnp.where(keeps_own, 1, 0)
     pl.semaphore_wait(barrier, greetings)
 
     def send_first(k, carry):
-        at = (sta + k) % KEPT
-        to = at // BANDS
-        place = keeper(at % BANDS * DAYS + day, to % 2)
+        to = (sta + k) % DAYS
+        to_band = (plane * BANDS // 8 + outward(k // DAYS, BANDS // 2)) % BANDS
+        at = to * BANDS + to_band
+        place = keeper(to_band * DAYS + day, to % 2)
 
         @pl.when(jnp.logical_or(place != sta, to != day))
         def _():
@@ -182,7 +182,7 @@
             lax.fori_loop(0, BLOCKS, pick, 0, unroll=8)
 
             def send_back(k, carry):
-                to = (sta + k) % BLOCKS
+                to = far_first(sta, k)
                 pltpu.make_async_remote_copy(
                     src_ref=picked.at[r, to], dst_ref=returned.at[r, origin * BANDS + band],
                     send_sem=back_send, recv_sem=back_recv.at[r],
@@ -193,7 +193,7 @@
             pltpu.make_async_copy(
                 picked.at[r, sta], returned.at[r, origin * BANDS + band], back_recv.at[r]
             ).start()
-            lax.fori_loop(1, BLOCKS, send_back, 0, unroll=7)
+            lax.fori_loop(0, BLOCKS - 1, send_back, 0, unroll=7)
 
     for k in range(1, DAYS):
         pltpu.make_async_copy(spectra.at[0], spectra.at[0], own_recv.at[k - 1]).wait()

time: 41.4 us -> 39.8 us (0.961)
  Pallas kernels: 39.8 us -> 38.2 us
    pallas_call x1, Pallas kernels: 39.8 us -> 38.2 us  [per_device(): pl.pallas_call(kernel, out_shape=jax.ShapeDtypeStruct((ROUNDS, 2, SPB, LA...]
where the time goes in v3:
time: 39.8 us; the launch traced here: 39.7 us
  Pallas kernels  38.2 us (96%)
  local copies, waits for them, and re-layouts  1.42 us (4%)
    pallas_call x1, Pallas kernels, per_device(): pl.pallas_call(kernel, out_shape=jax.ShapeDtypeStruct((ROUNDS, 2, SPB, LA...  38.2 us
    unnamed x1, local copies, waits for them, and re-layouts  1.42 us

profile of v3, /device:TPU:1, one launch (start us, length us, event | category | flops | bytes accessed | tf_op | source)
XLA Modules:
  0.0 39.7 jit_solution(7030899277201398504)
XLA Ops:
  0.0 38.2 %correlate.1 = bf16[3,2,8,512]{3,2,1,0:T(8,128)(2,1)} custom-call(bf16[64,2,640]{2,1,0:T(2,128)(2,1)} %bitcast.1, s32[3,64]{1,0:T(4,128)} %pairing_hbm.1, s32[512]{0:T(512)} %slot_hbm.1, bf16[2,1280,512]{2,1,0:T(8,128)(2,1)} %constant.2.clone.table_hbm), custom_call_target="tpu_custom_call" | custom-call | tf_op jit(solution)/shard_map/correlate/pallas_call | solution.py:295
  38.3 1.4 %copy.6 = bf16[3,2,8,512]{3,2,1,0:T(8,128)(2,1)} copy(bf16[3,2,8,512]{3,2,1,0:T(8,128)(2,1)} %correlate.1) | data formatting | bytes 98304

commit v4 on v3

--- a/solution.py
+++ b/solution.py
@@ -19,9 +19,13 @@
 SEG = 8
 DAYS = 4
 BLOCKS = 64
-BANDS = 10
-KEPT = BANDS * DAYS
-ROWS = 16
+PLANES = 8
+WIDE = 8
+BANDS = 8
+GROUPS = 5
+ROWS = 4
+HALVES = 2
+NEAR = 4
 LANES = 128
 PIECE = 32
 TILES = NFREQ // LANES
@@ -40,18 +44,13 @@
     return np.stack([high, low])
 
 
-def keeper(kept, core):
-    z, turn = kept // 5, kept % 5
-    return z * 8 + (turn + 3 * core + 2 * z) % 8
-
-
 def outward(k, half):
     return half + (k + 1) // 2 * (1 - 2 * (k % 2))
 
 
 def far_first(sta, k):
-    plane = (sta // 8 + outward(k // 8, 4)) % 8
-    return plane * 8 + (sta % 8 + k % 8 + 1) % 8
+    plane = (sta // WIDE + outward(k // WIDE, PLANES // 2)) % PLANES
+    return plane * WIDE + (sta % WIDE + k % WIDE + 1) % WIDE
 
 
 def kernel(
@@ -60,29 +59,24 @@
     load_sem, first_send, first_recv, back_send, back_recv, own_send, own_recv,
 ):
     sta, day = lax.axis_index("sta"), lax.axis_index("day")
-    plane = sta // 8
-    turn = (sta % 8 + 6 * plane + 5 * (day % 2)) % 8
-    is_keeper = turn < 5
-    kept = plane * 5 + turn
-    band, origin = kept // DAYS, kept % DAYS
-    keeps_own = jnp.logical_and(is_keeper, origin == day)
+    plane, band = sta // WIDE, sta % WIDE
+    origin = (plane + band) % DAYS
+    keeps_own = origin == day
 
     barrier = pltpu.get_barrier_semaphore()
 
     def greet(place, to_day):
         pl.semaphore_signal(barrier, inc=1, device_id=(place, to_day), device_id_type=MESH)
 
-    @pl.when(is_keeper)
+    def greet_block(k, carry):
+        greet(far_first(sta, k), origin)
+        return carry
+
+    lax.fori_loop(0, BLOCKS - 1, greet_block, 0, unroll=7)
+
+    @pl.when(jnp.logical_not(keeps_own))
     def _():
-        def greet_block(k, carry):
-            greet(far_first(sta, k), origin)
-            return carry
-
-        lax.fori_loop(0, BLOCKS - 1, greet_block, 0, unroll=7)
-
-        @pl.when(origin != day)
-        def _():
-            greet(sta, origin)
+        greet(sta, origin)
 
     for k in range(1, DAYS):
         greet(sta, (day + k) % DAYS)
@@ -123,7 +117,8 @@
         tile = jnp.concatenate(
             [pairs[to][:, g * LANES : (g + 1) * LANES] for g in range(4)], axis=0
         )
-        sent[to * BANDS : to * BANDS + 8] = tile.T.astype(jnp.bfloat16).reshape(8, ROWS, LANES)
+        tile = tile.T.astype(jnp.bfloat16).reshape(BANDS, GROUPS - 1, ROWS, LANES)
+        sent[to * BANDS : (to + 1) * BANDS, : GROUPS - 1] = tile
     rest = []
     for g in range(4):
         piece = jnp.zeros((PIECE, LANES), jnp.float32)
@@ -135,78 +130,98 @@
         rest.append(piece)
     rest = jnp.concatenate(rest, axis=0).T.astype(jnp.bfloat16)
     for to in range(DAYS):
-        sent[to * BANDS + 8 : (to + 1) * BANDS] = rest[to * PIECE : (to + 1) * PIECE].reshape(
-            2, ROWS, LANES
-        )
+        tile = rest[to * PIECE : (to + 1) * PIECE].reshape(BANDS, ROWS, LANES)
+        sent[to * BANDS : (to + 1) * BANDS, GROUPS - 1] = tile
 
     loads[2].wait()
-    greetings = KEPT + DAYS - 1 - jnp.where(keeps_own, 1, 0)
+    greetings = BLOCKS + DAYS - 1 - jnp.where(keeps_own, 1, 0)
     pl.semaphore_wait(barrier, greetings)
 
+    beside = day + 1 - 2 * (day % 2)
+    across = (day + 2) % DAYS
+
+    def send_own(from_day, to_day, i):
+        pltpu.make_async_remote_copy(
+            src_ref=spectra.at[from_day], dst_ref=spectra.at[from_day], send_sem=own_send, recv_sem=own_recv.at[i],
+            device_id=(sta, to_day), device_id_type=MESH,
+        ).start()
+
+    def wait_own(i):
+        pltpu.make_async_copy(spectra.at[0], spectra.at[0], own_recv.at[i]).wait()
+
+    def keep(from_day, square):
+        for c in range(2):
+            for seg in range(SEG):
+                x = natural[c, :, seg, :]
+                own[c, from_day, seg] = x
+                for t in range(TILES):
+                    x_t = x[:, t * LANES : (t + 1) * LANES]
+                    square = square + x_t * x_t
+        return square
+
+    send_own(day, across, 0)
+    send_own(day, beside, 1)
+
     def send_first(k, carry):
-        to = (sta + k) % DAYS
-        to_band = (plane * BANDS // 8 + outward(k // DAYS, BANDS // 2)) % BANDS
-        at = to * BANDS + to_band
-        place = keeper(to_band * DAYS + day, to % 2)
+        to_plane = (plane + outward(k // WIDE, PLANES // 2)) % PLANES
+        to_band = (day + PLANES - to_plane) % DAYS + k % HALVES * DAYS
+        to = k // HALVES % DAYS
+        place = to_plane * WIDE + to_band
 
         @pl.when(jnp.logical_or(place != sta, to != day))
         def _():
             pltpu.make_async_remote_copy(
-                src_ref=sent.at[at], dst_ref=banded.at[sta], send_sem=first_send, recv_sem=first_recv,
-                device_id=(place, to), device_id_type=MESH,
+                src_ref=sent.at[to * BANDS + to_band], dst_ref=banded.at[sta],
+                send_sem=first_send, recv_sem=first_recv, device_id=(place, to), device_id_type=MESH,
             ).start()
 
         return carry
 
-    lax.fori_loop(0, KEPT, send_first, 0, unroll=4)
+    lax.fori_loop(0, BLOCKS, send_first, 0, unroll=8)
 
     @pl.when(keeps_own)
     def _():
         pltpu.make_async_copy(sent.at[day * BANDS + band], banded.at[sta], first_recv).start()
 
-    for k in range(1, DAYS):
-        pltpu.make_async_remote_copy(
-            src_ref=spectra.at[day], dst_ref=spectra.at[day], send_sem=own_send, recv_sem=own_recv.at[k - 1],
-            device_id=(sta, (day + k) % DAYS), device_id_type=MESH,
-        ).start()
-
-    @pl.when(is_keeper)
-    def _():
-        pltpu.make_async_copy(banded, banded, first_recv).wait()
-        for r in range(ROUNDS):
-
-            def pick(b, carry):
-                picked[r, b] = banded[pairing_ref[r, b]]
-                return carry
-
-            lax.fori_loop(0, BLOCKS, pick, 0, unroll=8)
+    square = keep(day, jnp.zeros((SPB, LANES), jnp.float32))
+    wait_own(1)
+    split(beside)
+    square = keep(beside, square)
+    wait_own(0)
+    send_own(across, beside, 2)
+    split(across)
+    square = keep(across, square)
+
+    side = 2 * (day % 2) - 1
+    at = origin * BANDS + band
+    pltpu.make_async_copy(banded, banded, first_recv).wait()
+    for r in range(ROUNDS):
+        for i, offset in enumerate((2, 1, -1, 0)):
+            first_block = (plane + PLANES + offset * side) % PLANES * WIDE
+            for k in range(WIDE):
+                picked[r, i * WIDE + k] = banded[pairing_ref[r, first_block + k]]
 
             def send_back(k, carry):
-                to = far_first(sta, k)
+                wide = (band + k + 1) % WIDE
                 pltpu.make_async_remote_copy(
-                    src_ref=picked.at[r, to], dst_ref=returned.at[r, origin * BANDS + band],
+                    src_ref=picked.at[r, i * WIDE + wide], dst_ref=returned.at[r, at],
                     send_sem=back_send, recv_sem=back_recv.at[r],
-                    device_id=(to, day), device_id_type=MESH,
+                    device_id=(first_block + wide, day), device_id_type=MESH,
                 ).start()
                 return carry
 
-            pltpu.make_async_copy(
-                picked.at[r, sta], returned.at[r, origin * BANDS + band], back_recv.at[r]
-            ).start()
-            lax.fori_loop(0, BLOCKS - 1, send_back, 0, unroll=7)
-
-    for k in range(1, DAYS):
-        pltpu.make_async_copy(spectra.at[0], spectra.at[0], own_recv.at[k - 1]).wait()
-    square = jnp.zeros((SPB, LANES), jnp.float32)
-    for q in range(DAYS):
-        split(q)
-        for c in range(2):
-            for seg in range(SEG):
-                x = natural[c, :, seg, :]
-                own[c, q, seg] = x
-                for t in range(TILES):
-                    x_t = x[:, t * LANES : (t + 1) * LANES]
-                    square = square + x_t * x_t
+            if offset:
+                lax.fori_loop(0, WIDE, send_back, 0, unroll=True)
+            else:
+                pltpu.make_async_copy(
+                    picked.at[r, i * WIDE + band], returned.at[r, at], back_recv.at[r]
+                ).start()
+                lax.fori_loop(0, WIDE - 1, send_back, 0, unroll=True)
+
+    wait_own(2)
+    last = (beside + 2) % DAYS
+    split(last)
+    square = keep(last, square)
     count = float(SEG * DAYS * 2 * NFREQ)
     energy_i = jnp.sum(square, axis=1, keepdims=True) / count + EPS
 
@@ -215,13 +230,13 @@
     for r in range(ROUNDS):
         pltpu.make_async_copy(returned.at[r], returned.at[r], back_recv.at[r]).wait()
         for q in range(DAYS):
-            tile = returned[r, q * BANDS : q * BANDS + 8].reshape(LANES, LANES)
+            tile = returned[r, q * BANDS : (q + 1) * BANDS, : GROUPS - 1].reshape(LANES, LANES)
             tile = tile.astype(jnp.float32).T.reshape(4, 2, 2, SEG, LANES)
             for g in range(4):
                 partner[:, :, q, :, g * LANES : (g + 1) * LANES] = tile[g]
         rest = jnp.concatenate(
             [
-                returned[r, q * BANDS + 8 : (q + 1) * BANDS].reshape(PIECE, LANES)
+                returned[r, q * BANDS : (q + 1) * BANDS, GROUPS - 1].reshape(PIECE, LANES)
                 for q in range(DAYS)
             ],
             axis=0,
@@ -268,21 +283,18 @@
             scale = 1.0 / (jnp.sqrt(energy_j * energy_i) * np.float32(np.sqrt(count)))
             out_ref[r, j] = (raw[j * SPB : (j + 1) * SPB] * scale).astype(jnp.bfloat16)
 
-    @pl.when(keeps_own)
-    def _():
-        rest_sent = sent.at[pl.ds(0, KEPT - 1)]
-        pltpu.make_async_copy(rest_sent, rest_sent, first_send).wait()
+    tiles = DAYS * BANDS
+    pltpu.make_async_copy(sent, sent, first_send).wait()
+    rest_sent = sent.at[pl.ds(0, tiles - 1)]
+    pltpu.make_async_copy(rest_sent, rest_sent, first_send).wait()
 
     @pl.when(jnp.logical_not(keeps_own))
     def _():
-        pltpu.make_async_copy(sent, sent, first_send).wait()
-
-    @pl.when(is_keeper)
-    def _():
-        for r in range(ROUNDS):
-            rest_sent = picked.at[r, pl.ds(0, BLOCKS - 1)]
-            pltpu.make_async_copy(rest_sent, rest_sent, back_send).wait()
-
+        pltpu.make_async_copy(sent.at[0], sent.at[0], first_send).wait()
+
+    for r in range(ROUNDS):
+        rest_sent = picked.at[r, pl.ds(0, NEAR * WIDE - 1)]
+        pltpu.make_async_copy(rest_sent, rest_sent, back_send).wait()
     rest_sent = spectra.at[pl.ds(0, DAYS - 1)]
     pltpu.make_async_copy(rest_sent, rest_sent, own_send).wait()
 
@@ -303,10 +315,10 @@
             pltpu.SMEM(station_slot.shape, jnp.int32),
             pltpu.VMEM((2, SPB, SEG, NFREQ), f32),
             pltpu.VMEM((2, DAYS, SEG, SPB, NFREQ), f32),
-            pltpu.VMEM((KEPT, ROWS, LANES), bf16),
-            pltpu.VMEM((BLOCKS, ROWS, LANES), bf16),
-            pltpu.VMEM((ROUNDS, BLOCKS, ROWS, LANES), bf16),
-            pltpu.VMEM((ROUNDS, KEPT, ROWS, LANES), bf16),
+            pltpu.VMEM((DAYS * BANDS, GROUPS, ROWS, LANES), bf16),
+            pltpu.VMEM((BLOCKS, GROUPS, ROWS, LANES), bf16),
+            pltpu.VMEM((ROUNDS, NEAR * WIDE, GROUPS, ROWS, LANES), bf16),
+            pltpu.VMEM((ROUNDS, DAYS * BANDS, GROUPS, ROWS, LANES), bf16),
             pltpu.VMEM((2, 2, DAYS, SEG, NFREQ), f32),
             pltpu.VMEM((2 * SPB, 2 * NFREQ), f32),
             pltpu.VMEM((2, 2 * NFREQ, LAGS), bf16),

time: 39.8 us -> 38.3 us (0.962)
  Pallas kernels: 38.2 us -> 36.7 us
    pallas_call x1, Pallas kernels: 38.2 us -> 36.7 us  [per_device(): pl.pallas_call(kernel, out_shape=jax.ShapeDtypeStruct((ROUNDS, 2, SPB, LA...]
where the time goes in v4:
time: 38.3 us; the launch traced here: 38.2 us
  Pallas kernels  36.7 us (96%)
  local copies, waits for them, and re-layouts  1.42 us (4%)
    pallas_call x1, Pallas kernels, per_device(): pl.pallas_call(kernel, out_shape=jax.ShapeDtypeStruct((ROUNDS, 2, SPB, LA...  36.7 us
    unnamed x1, local copies, waits for them, and re-layouts  1.42 us

profile of v4, /device:TPU:1, one launch (start us, length us, event | category | flops | bytes accessed | tf_op | source)
XLA Modules:
  0.0 38.2 jit_solution(3891081628074404976)
XLA Ops:
  0.0 36.7 %correlate.1 = bf16[3,2,8,512]{3,2,1,0:T(8,128)(2,1)} custom-call(bf16[64,2,640]{2,1,0:T(2,128)(2,1)} %bitcast.1, s32[3,64]{1,0:T(4,128)} %pairing_hbm.1, s32[512]{0:T(512)} %slot_hbm.1, bf16[2,1280,512]{2,1,0:T(8,128)(2,1)} %constant.2.clone.table_hbm), custom_call_target="tpu_custom_call" | custom-call | tf_op jit(solution)/shard_map/correlate/pallas_call | solution.py:307
  36.7 1.4 %copy.6 = bf16[3,2,8,512]{3,2,1,0:T(8,128)(2,1)} copy(bf16[3,2,8,512]{3,2,1,0:T(8,128)(2,1)} %correlate.1) | data formatting | bytes 98304

commit v5 on v4

--- a/solution.py
+++ b/solution.py
@@ -54,8 +54,8 @@
 
 
 def kernel(
-    x_hbm, pairing_hbm, slot_hbm, table_hbm, out_ref,
-    spectra, pairing_ref, slot_ref, natural, own, sent, banded, picked, returned, partner, cross, table,
+    x_hbm, plan_hbm, table_hbm, out_ref,
+    spectra, plan_ref, natural, own, sent, banded, picked, returned, partner, cross, table,
     load_sem, first_send, first_recv, back_send, back_recv, own_send, own_recv,
 ):
     sta, day = lax.axis_index("sta"), lax.axis_index("day")
@@ -84,7 +84,7 @@
     loads = [
         pltpu.make_async_copy(source, target, load_sem.at[i])
         for i, (source, target) in enumerate(
-            [(x_hbm, spectra.at[day]), (slot_hbm, slot_ref), (pairing_hbm, pairing_ref), (table_hbm, table)]
+            [(x_hbm, spectra.at[day]), (plan_hbm, plan_ref), (table_hbm, table)]
         )
     ]
     for load in loads:
@@ -99,7 +99,7 @@
             natural[c] = part.reshape(SPB, SEG, NFREQ)
 
     split(day)
-    slots = [slot_ref[sta * SPB + i] for i in range(SPB)]
+    slots = [plan_ref[ROUNDS, sta * SPB + i] for i in range(SPB)]
     order = []
     for j in range(SPB):
         at = jnp.int32(0)
@@ -133,16 +133,15 @@
         tile = rest[to * PIECE : (to + 1) * PIECE].reshape(BANDS, ROWS, LANES)
         sent[to * BANDS : (to + 1) * BANDS, GROUPS - 1] = tile
 
-    loads[2].wait()
     greetings = BLOCKS + DAYS - 1 - jnp.where(keeps_own, 1, 0)
     pl.semaphore_wait(barrier, greetings)
 
     beside = day + 1 - 2 * (day % 2)
     across = (day + 2) % DAYS
 
-    def send_own(from_day, to_day, i):
+    def send_own(from_day, to_day, i, part=slice(None)):
         pltpu.make_async_remote_copy(
-            src_ref=spectra.at[from_day], dst_ref=spectra.at[from_day], send_sem=own_send, recv_sem=own_recv.at[i],
+            src_ref=spectra.at[from_day, part], dst_ref=spectra.at[from_day, part], send_sem=own_send, recv_sem=own_recv.at[i],
             device_id=(sta, to_day), device_id_type=MESH,
         ).start()
 
@@ -159,13 +158,13 @@
                     square = square + x_t * x_t
         return square
 
-    send_own(day, across, 0)
     send_own(day, beside, 1)
 
     def send_first(k, carry):
-        to_plane = (plane + outward(k // WIDE, PLANES // 2)) % PLANES
-        to_band = (day + PLANES - to_plane) % DAYS + k % HALVES * DAYS
-        to = k // HALVES % DAYS
+        to_plane = (plane + 1 + k // WIDE) % PLANES
+        turn = (k + band) % WIDE
+        to_band = (day + PLANES - to_plane) % DAYS + turn % HALVES * DAYS
+        to = turn // HALVES
         place = to_plane * WIDE + to_band
 
         @pl.when(jnp.logical_or(place != sta, to != day))
@@ -177,7 +176,9 @@
 
         return carry
 
-    lax.fori_loop(0, BLOCKS, send_first, 0, unroll=8)
+    for i in range(PLANES):
+        lax.fori_loop(i * WIDE, (i + 1) * WIDE, send_first, 0, unroll=True)
+        send_own(day, across, 0, pl.ds(i * SPB, SPB))
 
     @pl.when(keeps_own)
     def _():
@@ -199,7 +200,7 @@
         for i, offset in enumerate((2, 1, -1, 0)):
             first_block = (plane + PLANES + offset * side) % PLANES * WIDE
             for k in range(WIDE):
-                picked[r, i * WIDE + k] = banded[pairing_ref[r, first_block + k]]
+                picked[r, i * WIDE + k] = banded[plan_ref[r, first_block + k]]
 
             def send_back(k, carry):
                 wide = (band + k + 1) % WIDE
@@ -225,7 +226,7 @@
     count = float(SEG * DAYS * 2 * NFREQ)
     energy_i = jnp.sum(square, axis=1, keepdims=True) / count + EPS
 
-    loads[3].wait()
+    loads[2].wait()
     dot = functools.partial(jnp.dot, preferred_element_type=jnp.float32)
     for r in range(ROUNDS):
         pltpu.make_async_copy(returned.at[r], returned.at[r], back_recv.at[r]).wait()
@@ -301,18 +302,19 @@
 
 def per_device(spectra, pairing, station_slot):
     x = spectra.reshape(SPB * SEG, 2, NFREQ)
+    wide = jnp.pad(pairing, ((0, 0), (0, station_slot.size - BLOCKS)))
+    plan = jnp.concatenate([wide, station_slot[None]], axis=0)
     hbm = pl.BlockSpec(memory_space=pltpu.HBM)
     dma = pltpu.SemaphoreType.DMA
     f32, bf16 = jnp.float32, jnp.bfloat16
     return pl.pallas_call(
         kernel,
         out_shape=jax.ShapeDtypeStruct((ROUNDS, 2, SPB, LAGS), bf16),
-        in_specs=[hbm] * 4,
+        in_specs=[hbm] * 3,
         out_specs=pl.BlockSpec(memory_space=pltpu.VMEM),
         scratch_shapes=[
             pltpu.VMEM((DAYS,) + x.shape, bf16),
-            pltpu.SMEM(pairing.shape, jnp.int32),
-            pltpu.SMEM(station_slot.shape, jnp.int32),
+            pltpu.SMEM(plan.shape, jnp.int32),
             pltpu.VMEM((2, SPB, SEG, NFREQ), f32),
             pltpu.VMEM((2, DAYS, SEG, SPB, NFREQ), f32),
             pltpu.VMEM((DAYS * BANDS, GROUPS, ROWS, LANES), bf16),
@@ -322,13 +324,13 @@
             pltpu.VMEM((2, 2, DAYS, SEG, NFREQ), f32),
             pltpu.VMEM((2 * SPB, 2 * NFREQ), f32),
             pltpu.VMEM((2, 2 * NFREQ, LAGS), bf16),
-            dma((4,)), dma, dma, dma, dma((ROUNDS,)), dma, dma((DAYS - 1,)),
+            dma((3,)), dma, dma, dma, dma((ROUNDS,)), dma, dma((DAYS - 1,)),
         ],
         compiler_params=pltpu.CompilerParams(
-            collective_id=0, has_side_effects=True, vmem_limit_bytes=63 * 1024 * 1024
+            collective_id=0, has_side_effects=True, vmem_limit_bytes=55168 * 1024
         ),
         name="correlate",
-    )(x, pairing, station_slot, jnp.asarray(lag_table()))
+    )(x, plan, jnp.asarray(lag_table()))
 
 
 def solution(mesh):

time: 38.3 us -> 36.8 us (0.961)
  Pallas kernels: 36.7 us -> 35.3 us
  local copies, waits for them, and re-layouts: 1.42 us -> 0.62 us
  other arithmetic: 0 us -> 0.71 us
    pallas_call x1, Pallas kernels: 36.7 us -> 35.3 us  [per_device(): pl.pallas_call(kernel, out_shape=jax.ShapeDtypeStruct((ROUNDS, 2, SPB, LA...]
    unnamed x1, local copies, waits for them, and re-layouts: 1.42 us -> 0.62 us
    concatenate x0 -> x1, other arithmetic: none -> 0.71 us  [per_device(): plan = jnp.concatenate([wide, station_slot[None]], axis=0)]
where the time goes in v5:
time: 36.8 us; the launch traced here: 36.6 us
  Pallas kernels  35.3 us (96%)
  other arithmetic  0.71 us (2%)
  local copies, waits for them, and re-layouts  0.62 us (2%)
    pallas_call x1, Pallas kernels, per_device(): pl.pallas_call(kernel, out_shape=jax.ShapeDtypeStruct((ROUNDS, 2, SPB, LA...  35.3 us

profile of v5, /device:TPU:1, one launch (start us, length us, event | category | flops | bytes accessed | tf_op | source)
XLA Modules:
  0.0 36.6 jit_solution(2194850189093137368)
XLA Ops:
  0.0 0.7 %pad_add_fusion.plan_hbm = s32[4,512]{1,0:T(4,128)S(1)} fusion(s32[3,64]{1,0:T(4,128)} %param.5, s32[1,512]{1,0:T(1,128)} %bitcast.3), kind=kLoop, calls=%fused_computation | loop fusion | flops 2048 | bytes 11008 | tf_op jit(solution)/shard_map/concatenate | solution.py:306
  0.7 35.3 %correlate.1 = bf16[3,2,8,512]{3,2,1,0:T(8,128)(2,1)S(1)} custom-call(bf16[64,2,640]{2,1,0:T(2,128)(2,1)} %bitcast.2, s32[4,512]{1,0:T(4,128)S(1)} %pad_add_fusion.plan_hbm, bf16[2,1280,512]{2,1,0:T(8,128)(2,1)} %constant.4.clone.table_hbm), custom_call_target="tpu_custom_call" | custom-call | tf_op jit(solution)/shard_map/correlate/pallas_call | solution.py:310
  36.0 0.6 %copy.6 = bf16[3,2,8,512]{3,2,1,0:T(8,128)(2,1)} copy(bf16[3,2,8,512]{3,2,1,0:T(8,128)(2,1)S(1)} %correlate.1) | data formatting | bytes 98304

commit v6 on v5

--- a/solution.py
+++ b/solution.py
@@ -31,14 +31,17 @@
 TILES = NFREQ // LANES
 WHOLE = 512
 MESH = pl.DeviceIdType.MESH
+ORDER = sorted(
+    ((r, i) for r in range(ROUNDS) for i in range(NEAR)), key=lambda at: (at[0], at[1])
+)
 
 
 def lag_table():
     bins = BIN_LO + np.arange(NFREQ, dtype=np.int64)
-    shifts = np.arange(LAGS, dtype=np.int64) - LAGS // 2
-    turns = np.mod(bins[:, None] * shifts[None, :], SEGLEN)
-    angle = 2.0 * np.pi / SEGLEN * turns
-    table = np.concatenate([np.cos(angle), -np.sin(angle)], axis=0).astype(np.float32)
+    halves = 2 * np.arange(LAGS // 2, dtype=np.int64) + 1
+    turns = np.mod(bins[:, None] * halves[None, :], 2 * SEGLEN)
+    angle = np.pi / SEGLEN * turns
+    table = np.stack([np.cos(angle), np.sin(angle)]).astype(np.float32)
     high = table.astype(ml_dtypes.bfloat16)
     low = (table - high.astype(np.float32)).astype(ml_dtypes.bfloat16)
     return np.stack([high, low])
@@ -190,35 +193,39 @@
     square = keep(beside, square)
     wait_own(0)
     send_own(across, beside, 2)
+
+    at = origin * BANDS + band
+    pltpu.make_async_copy(banded, banded, first_recv).wait()
+    first_plane = (plane + PLANES - 2 + day % 2) % PLANES
+    wrapped = jnp.maximum(first_plane + NEAR - PLANES, 0)
+    for r, i in ORDER:
+        to_plane = (first_plane + (NEAR - wrapped + i) % NEAR) % PLANES
+        for k in range(WIDE):
+            picked[r, i * WIDE + k] = banded[plan_ref[r, to_plane * WIDE + k]]
+
+        def send_back(k, carry):
+            wide = (band + k + 1) % WIDE
+            pltpu.make_async_remote_copy(
+                src_ref=picked.at[r, i * WIDE + wide], dst_ref=returned.at[r, at],
+                send_sem=back_send, recv_sem=back_recv.at[r],
+                device_id=(to_plane * WIDE + wide, day), device_id_type=MESH,
+            ).start()
+            return carry
+
+        lax.fori_loop(0, WIDE - 1, send_back, 0, unroll=True)
+
+        @pl.when(to_plane != plane)
+        def _():
+            send_back(WIDE - 1, 0)
+
+        @pl.when(to_plane == plane)
+        def _():
+            pltpu.make_async_copy(
+                picked.at[r, i * WIDE + band], returned.at[r, at], back_recv.at[r]
+            ).start()
+
     split(across)
     square = keep(across, square)
-
-    side = 2 * (day % 2) - 1
-    at = origin * BANDS + band
-    pltpu.make_async_copy(banded, banded, first_recv).wait()
-    for r in range(ROUNDS):
-        for i, offset in enumerate((2, 1, -1, 0)):
-            first_block = (plane + PLANES + offset * side) % PLANES * WIDE
-            for k in range(WIDE):
-                picked[r, i * WIDE + k] = banded[plan_ref[r, first_block + k]]
-
-            def send_back(k, carry):
-                wide = (band + k + 1) % WIDE
-                pltpu.make_async_remote_copy(
-                    src_ref=picked.at[r, i * WIDE + wide], dst_ref=returned.at[r, at],
-                    send_sem=back_send, recv_sem=back_recv.at[r],
-                    device_id=(first_block + wide, day), device_id_type=MESH,
-                ).start()
-                return carry
-
-            if offset:
-                lax.fori_loop(0, WIDE, send_back, 0, unroll=True)
-            else:
-                pltpu.make_async_copy(
-                    picked.at[r, i * WIDE + band], returned.at[r, at], back_recv.at[r]
-                ).start()
-                lax.fori_loop(0, WIDE - 1, send_back, 0, unroll=True)
-
     wait_own(2)
     last = (beside + 2) % DAYS
     split(last)
@@ -228,6 +235,14 @@
 
     loads[2].wait()
     dot = functools.partial(jnp.dot, preferred_element_type=jnp.float32)
+    bins = BIN_LO + lax.broadcasted_iota(jnp.int32, (SPB, NFREQ), 1)
+    half = bins.astype(jnp.float32) * np.float32(np.pi / SEGLEN)
+    half_cos, half_sin = jnp.cos(half), jnp.sin(half)
+    backward = LANES - 1 - lax.broadcasted_iota(jnp.int32, (2 * SPB, LANES), 1)
+
+    def mirrored(tile):
+        return jnp.take_along_axis(tile, backward, axis=1)
+
     for r in range(ROUNDS):
         pltpu.make_async_copy(returned.at[r], returned.at[r], back_recv.at[r]).wait()
         for q in range(DAYS):
@@ -266,12 +281,19 @@
         zero = jnp.zeros((SPB, NFREQ), jnp.float32)
         sums = lax.fori_loop(0, DAYS, correlate, (zero,) * 4)
         for j in range(2):
-            for c in range(2):
-                cross[j * SPB : (j + 1) * SPB, c * NFREQ : (c + 1) * NFREQ] = sums[2 * j + c]
-        spectrum = cross[...]
-        high = spectrum.astype(jnp.bfloat16)
-        low = (spectrum - high.astype(jnp.float32)).astype(jnp.bfloat16)
-        raw = dot(high, table[0]) + dot(low, table[0]) + dot(high, table[1])
+            real, imag = sums[2 * j], sums[2 * j + 1]
+            cross[0, j * SPB : (j + 1) * SPB] = real * half_cos + imag * half_sin
+            cross[1, j * SPB : (j + 1) * SPB] = imag * half_cos - real * half_sin
+        waves = []
+        for c in range(2):
+            high = cross[c].astype(jnp.bfloat16)
+            low = (cross[c] - high.astype(jnp.float32)).astype(jnp.bfloat16)
+            both = dot(jnp.concatenate([high, low], axis=0), table[0, c])
+            waves.append(both[: 2 * SPB] + both[2 * SPB :] + dot(high, table[1, c]))
+        early, late = waves[0] + waves[1], waves[0] - waves[1]
+        raw = jnp.concatenate(
+            [mirrored(early[:, LANES:]), mirrored(early[:, :LANES]), late], axis=1
+        )
         for j in range(2):
             square = jnp.zeros((SEG, LANES), jnp.float32)
             for c in range(2):
@@ -322,8 +344,8 @@
             pltpu.VMEM((ROUNDS, NEAR * WIDE, GROUPS, ROWS, LANES), bf16),
             pltpu.VMEM((ROUNDS, DAYS * BANDS, GROUPS, ROWS, LANES), bf16),
             pltpu.VMEM((2, 2, DAYS, SEG, NFREQ), f32),
-            pltpu.VMEM((2 * SPB, 2 * NFREQ), f32),
-            pltpu.VMEM((2, 2 * NFREQ, LAGS), bf16),
+            pltpu.VMEM((2, 2 * SPB, NFREQ), f32),
+            pltpu.VMEM((2, 2, NFREQ, LAGS // 2), bf16),
             dma((3,)), dma, dma, dma, dma((ROUNDS,)), dma, dma((DAYS - 1,)),
         ],
         compiler_params=pltpu.CompilerParams(

time: 36.8 us -> 35.8 us (0.973)
  Pallas kernels: 35.3 us -> 34.1 us
    pallas_call x1, Pallas kernels: 35.3 us -> 34.1 us  [per_device(): pl.pallas_call(kernel, out_shape=jax.ShapeDtypeStruct((ROUNDS, 2, SPB, LA...]
where the time goes in v6:
time: 35.8 us; the launch traced here: 35.5 us
  Pallas kernels  34.1 us (95%)
  other arithmetic  0.71 us (2%)
  local copies, waits for them, and re-layouts  0.62 us (2%)
    pallas_call x1, Pallas kernels, per_device(): pl.pallas_call(kernel, out_shape=jax.ShapeDtypeStruct((ROUNDS, 2, SPB, LA...  34.1 us

profile of v6, /device:TPU:1, one launch (start us, length us, event | category | flops | bytes accessed | tf_op | source)
XLA Modules:
  0.0 35.5 jit_solution(10141068695728706712)
XLA Ops:
  0.0 0.7 %pad_add_fusion.plan_hbm = s32[4,512]{1,0:T(4,128)S(1)} fusion(s32[3,64]{1,0:T(4,128)} %param.5, s32[1,512]{1,0:T(1,128)} %bitcast.3), kind=kLoop, calls=%fused_computation | loop fusion | flops 2048 | bytes 11008 | tf_op jit(solution)/shard_map/concatenate | solution.py:328
  0.7 34.1 %correlate.1 = bf16[3,2,8,512]{3,2,1,0:T(8,128)(2,1)S(1)} custom-call(bf16[64,2,640]{2,1,0:T(2,128)(2,1)} %bitcast.2, s32[4,512]{1,0:T(4,128)S(1)} %pad_add_fusion.plan_hbm, bf16[2,2,640,256]{3,2,1,0:T(8,128)(2,1)} %constant.4.clone.table_hbm), custom_call_target="tpu_custom_call" | custom-call | tf_op jit(solution)/shard_map/correlate/pallas_call | solution.py:332
  34.9 0.6 %copy.6 = bf16[3,2,8,512]{3,2,1,0:T(8,128)(2,1)} copy(bf16[3,2,8,512]{3,2,1,0:T(8,128)(2,1)S(1)} %correlate.1) | data formatting | bytes 98304

commit v7 on v6

--- a/solution.py
+++ b/solution.py
@@ -31,9 +31,6 @@
 TILES = NFREQ // LANES
 WHOLE = 512
 MESH = pl.DeviceIdType.MESH
-ORDER = sorted(
-    ((r, i) for r in range(ROUNDS) for i in range(NEAR)), key=lambda at: (at[0], at[1])
-)
 
 
 def lag_table():
@@ -164,7 +161,9 @@
     send_own(day, beside, 1)
 
     def send_first(k, carry):
-        to_plane = (plane + 1 + k // WIDE) % PLANES
+        step = k // WIDE
+        to_plane = PLANES + (step // 2 + 1) * (1 - 2 * (step % 2)) + step // (PLANES - 1) * DAYS
+        to_plane = (plane + to_plane) % PLANES
         turn = (k + band) % WIDE
         to_band = (day + PLANES - to_plane) % DAYS + turn % HALVES * DAYS
         to = turn // HALVES
@@ -198,31 +197,35 @@
     pltpu.make_async_copy(banded, banded, first_recv).wait()
     first_plane = (plane + PLANES - 2 + day % 2) % PLANES
     wrapped = jnp.maximum(first_plane + NEAR - PLANES, 0)
-    for r, i in ORDER:
-        to_plane = (first_plane + (NEAR - wrapped + i) % NEAR) % PLANES
-        for k in range(WIDE):
-            picked[r, i * WIDE + k] = banded[plan_ref[r, to_plane * WIDE + k]]
-
-        def send_back(k, carry):
-            wide = (band + k + 1) % WIDE
-            pltpu.make_async_remote_copy(
-                src_ref=picked.at[r, i * WIDE + wide], dst_ref=returned.at[r, at],
-                send_sem=back_send, recv_sem=back_recv.at[r],
-                device_id=(to_plane * WIDE + wide, day), device_id_type=MESH,
-            ).start()
-            return carry
-
-        lax.fori_loop(0, WIDE - 1, send_back, 0, unroll=True)
-
-        @pl.when(to_plane != plane)
-        def _():
-            send_back(WIDE - 1, 0)
-
-        @pl.when(to_plane == plane)
-        def _():
-            pltpu.make_async_copy(
-                picked.at[r, i * WIDE + band], returned.at[r, at], back_recv.at[r]
-            ).start()
+    def serve(r, carry):
+        for i in range(NEAR):
+            to_plane = (first_plane + (NEAR - wrapped + i) % NEAR) % PLANES
+            for k in range(WIDE):
+                picked[r, i * WIDE + k] = banded[plan_ref[r, to_plane * WIDE + k]]
+
+            def send_back(k, carry):
+                wide = (band + k + 1) % WIDE
+                pltpu.make_async_remote_copy(
+                    src_ref=picked.at[r, i * WIDE + wide], dst_ref=returned.at[r, at],
+                    send_sem=back_send, recv_sem=back_recv.at[r],
+                    device_id=(to_plane * WIDE + wide, day), device_id_type=MESH,
+                ).start()
+                return carry
+
+            lax.fori_loop(0, WIDE - 1, send_back, 0, unroll=True)
+
+            @pl.when(to_plane != plane)
+            def _():
+                send_back(WIDE - 1, 0)
+
+            @pl.when(to_plane == plane)
+            def _():
+                pltpu.make_async_copy(
+                    picked.at[r, i * WIDE + band], returned.at[r, at], back_recv.at[r]
+                ).start()
+        return carry
+
+    lax.fori_loop(0, ROUNDS, serve, 0)
 
     split(across)
     square = keep(across, square)
@@ -243,7 +246,7 @@
     def mirrored(tile):
         return jnp.take_along_axis(tile, backward, axis=1)
 
-    for r in range(ROUNDS):
+    def finish(r, carry):
         pltpu.make_async_copy(returned.at[r], returned.at[r], back_recv.at[r]).wait()
         for q in range(DAYS):
             tile = returned[r, q * BANDS : (q + 1) * BANDS, : GROUPS - 1].reshape(LANES, LANES)
@@ -305,6 +308,9 @@
             energy_j = jnp.sum(energy_j, axis=0, keepdims=True) / count + EPS
             scale = 1.0 / (jnp.sqrt(energy_j * energy_i) * np.float32(np.sqrt(count)))
             out_ref[r, j] = (raw[j * SPB : (j + 1) * SPB] * scale).astype(jnp.bfloat16)
+        return carry
+
+    lax.fori_loop(0, ROUNDS, finish, 0)
 
     tiles = DAYS * BANDS
     pltpu.make_async_copy(sent, sent, first_send).wait()

time: 35.8 us -> 35.8 us (level)
  no operation moved by 1% of the time
where the time goes in v7:
time: 35.8 us; the launch traced here: 35.6 us
  Pallas kernels  34.3 us (96%)
  other arithmetic  0.71 us (2%)
  local copies, waits for them, and re-layouts  0.62 us (2%)
    pallas_call x1, Pallas kernels, per_device(): pl.pallas_call(kernel, out_shape=jax.ShapeDtypeStruct((ROUNDS, 2, SPB, LA...  34.3 us

profile of v7, /device:TPU:1, one launch (start us, length us, event | category | flops | bytes accessed | tf_op | source)
XLA Modules:
  0.0 35.6 jit_solution(8240393762738834120)
XLA Ops:
  0.0 0.7 %pad_add_fusion.plan_hbm = s32[4,512]{1,0:T(4,128)S(1)} fusion(s32[3,64]{1,0:T(4,128)} %param.5, s32[1,512]{1,0:T(1,128)} %bitcast.3), kind=kLoop, calls=%fused_computation | loop fusion | flops 2048 | bytes 11008 | tf_op jit(solution)/shard_map/concatenate | solution.py:334
  0.7 34.3 %correlate.1 = bf16[3,2,8,512]{3,2,1,0:T(8,128)(2,1)S(1)} custom-call(bf16[64,2,640]{2,1,0:T(2,128)(2,1)} %bitcast.2, s32[4,512]{1,0:T(4,128)S(1)} %pad_add_fusion.plan_hbm, bf16[2,2,640,256]{3,2,1,0:T(8,128)(2,1)} %constant.4.clone.table_hbm), custom_call_target="tpu_custom_call" | custom-call | tf_op jit(solution)/shard_map/correlate/pallas_call | solution.py:338
  35.0 0.6 %copy.6 = bf16[3,2,8,512]{3,2,1,0:T(8,128)(2,1)} copy(bf16[3,2,8,512]{3,2,1,0:T(8,128)(2,1)S(1)} %correlate.1) | data formatting | bytes 98304

commit v8 on v6

--- a/solution.py
+++ b/solution.py
@@ -164,7 +164,8 @@
     send_own(day, beside, 1)
 
     def send_first(k, carry):
-        to_plane = (plane + 1 + k // WIDE) % PLANES
+        i_plane = k // WIDE
+        to_plane = (plane + PLANES + (i_plane // 2 + 1) * (1 - 2 * (i_plane % 2)) + i_plane // 7 * 4) % PLANES
         turn = (k + band) % WIDE
         to_band = (day + PLANES - to_plane) % DAYS + turn % HALVES * DAYS
         to = turn // HALVES

time: 35.8 us -> 35.8 us (level)
  no operation moved by 1% of the time
where the time goes in v8:
time: 35.8 us; the launch traced here: 35.6 us
  Pallas kernels  34.3 us (96%)
  other arithmetic  0.71 us (2%)
  local copies, waits for them, and re-layouts  0.62 us (2%)
    pallas_call x1, Pallas kernels, per_device(): pl.pallas_call(kernel, out_shape=jax.ShapeDtypeStruct((ROUNDS, 2, SPB, LA...  34.3 us

profile of v8, /device:TPU:1, one launch (start us, length us, event | category | flops | bytes accessed | tf_op | source)
XLA Modules:
  0.0 35.6 jit_solution(4044867786978893325)
XLA Ops:
  0.0 0.7 %pad_add_fusion.plan_hbm = s32[4,512]{1,0:T(4,128)S(1)} fusion(s32[3,64]{1,0:T(4,128)} %param.5, s32[1,512]{1,0:T(1,128)} %bitcast.3), kind=kLoop, calls=%fused_computation | loop fusion | flops 2048 | bytes 11008 | tf_op jit(solution)/shard_map/concatenate | solution.py:329
  0.7 34.3 %correlate.1 = bf16[3,2,8,512]{3,2,1,0:T(8,128)(2,1)S(1)} custom-call(bf16[64,2,640]{2,1,0:T(2,128)(2,1)} %bitcast.2, s32[4,512]{1,0:T(4,128)S(1)} %pad_add_fusion.plan_hbm, bf16[2,2,640,256]{3,2,1,0:T(8,128)(2,1)} %constant.4.clone.table_hbm), custom_call_target="tpu_custom_call" | custom-call | tf_op jit(solution)/shard_map/correlate/pallas_call | solution.py:333
  35.0 0.6 %copy.6 = bf16[3,2,8,512]{3,2,1,0:T(8,128)(2,1)} copy(bf16[3,2,8,512]{3,2,1,0:T(8,128)(2,1)S(1)} %correlate.1) | data formatting | bytes 98304
